TPU v7x, 512 devices: a whole 4x8x8 slice. The times are simulated.
512 devices in a mesh: section: 32 (over z, x), tensor: 16 (over y, core).
Axes of the slice: x: 4, y: 8, z: 8, core: 2. Of those that a mesh axis runs over, the one named last changes fastest.
Arguments:
- travelling_activation: bfloat16 [32, 64, 6144], P('section', None, 'tensor'), may hold values from -45 to 45
- entering: bfloat16 [1, 64, 6144], P(None, None, 'tensor'), may hold values from -45 to 45
- stashed: bfloat16 [32, 2, 64, 6144], P('section', None, None, 'tensor'), may hold values from -45 to 45
- travelling_gradient: bfloat16 [32, 64, 6144], P('section', None, 'tensor'), may hold values from -45 to 45
- returning: bfloat16 [1, 64, 6144], P(None, None, 'tensor'), may hold values from -45 to 45
- frozen: bfloat16 [32, 6144, 6144], P('section', None, 'tensor'), may hold values from -4 to 4
- input_projection: bfloat16 [32, 16, 6144], P('section', None, 'tensor'), may hold values from -0.3125 to 0.3125
- output_projection: bfloat16 [32, 16, 6144], P('section', None, 'tensor'), may hold values from -0.3125 to 0.3125
- magnitude: float32 [32, 6144], P('section', 'tensor'), may hold values from 0.5 to 2
- input_norm_gain: bfloat16 [32, 6144], P('section', 'tensor'), may hold values from 0.5 to 1.5
Outputs:
- act_out: bfloat16 [32, 64, 6144], P('section', None, 'tensor')
- grad_out: bfloat16 [32, 64, 6144], P('section', None, 'tensor')
- grad_mag: float32 [32, 6144], P('section', 'tensor')
- grad_in: float32 [32, 16, 6144], P('section', None, 'tensor')
- grad_outproj: float32 [32, 16, 6144], P('section', None, 'tensor')
- gain_grad: float32 [32, 6144], P('section', 'tensor')
All inputs are finite; a program needn't handle non-finite values.
Results may differ from a plain program's by a relative error of at most 0.034.
Values may be sent and summed in bfloat16 or wider, within the bound.
A program may use at most 128 MiB of HBM per device.

v0:
```python
import jax
import jax.numpy as jnp
from jax import lax
from jax.sharding import PartitionSpec as P


def shifted(block, axis, distance):
    devices = range(lax.axis_size(axis))
    route = [(i - distance, i) for i in devices if i - distance in devices]
    return lax.ppermute(block, axis, route)


def local(
    travelling_activation,
    entering,
    stashed,
    travelling_gradient,
    returning,
    frozen,
    input_projection,
    output_projection,
    magnitude,
    input_norm_gain,
):
    features = frozen.shape[1]
    columns = frozen.shape[2]
    slot_count = stashed.shape[1]
    row_count = stashed.shape[2]
    section_index = lax.axis_index("section")
    final_section = lax.axis_size("section") - 1
    gain_row = input_norm_gain[0].astype(jnp.float32)
    adapter_full = lax.all_gather(input_projection[0], "tensor", axis=1, tiled=True)
    direction = frozen[0].astype(jnp.float32) + jnp.einsum(
        "rd,rc->dc", adapter_full, output_projection[0], preferred_element_type=jnp.float32
    )
    colnorm = jnp.sqrt(jnp.sum(direction * direction, axis=0) + 1e-06)
    col_scale = magnitude[0] / colnorm
    merged = (direction * col_scale).astype(jnp.bfloat16)
    hidden_activation = travelling_activation[0]
    incoming_cotangent = travelling_gradient[0]
    emitted_rows = hidden_activation
    returned_gradient = incoming_cotangent
    normed_list = []
    pregrad_list = []
    gain_total = jnp.zeros((columns,), jnp.float32)
    for slot_index in range(slot_count):
        if slot_index > 0:
            arrived = shifted(emitted_rows, "section", 1)
            hidden_activation = jnp.where(section_index == 0, entering[slot_index - 1], arrived)
            returned = shifted(returned_gradient, "section", -1)
            incoming_cotangent = jnp.where(
                section_index == final_section, returning[slot_index - 1], returned
            )
        forward_inputs32 = hidden_activation.astype(jnp.float32)
        forward_squares = lax.psum(jnp.sum(forward_inputs32 * forward_inputs32, axis=-1), "tensor")
        forward_rscale = lax.rsqrt(forward_squares[:, None] / features + 1e-05)
        forward_normed = (forward_inputs32 * forward_rscale * gain_row).astype(jnp.bfloat16)
        forward_preact = jnp.dot(
            lax.all_gather(forward_normed, "tensor", axis=1, tiled=True),
            merged,
            preferred_element_type=jnp.float32,
        )
        emitted_rows = (forward_inputs32 + jax.nn.silu(forward_preact)).astype(jnp.bfloat16)
        prepare_inputs32 = stashed[0, slot_index].astype(jnp.float32)
        squares = lax.psum(jnp.sum(prepare_inputs32 * prepare_inputs32, axis=-1), "tensor")
        prepare_rscale = lax.rsqrt(squares[:, None] / features + 1e-05)
        prepare_normed = (prepare_inputs32 * prepare_rscale * gain_row).astype(jnp.bfloat16)
        prepare_normed_full = lax.all_gather(prepare_normed, "tensor", axis=1, tiled=True)
        inputs32 = stashed[0, slot_index].astype(jnp.float32)
        normed_full = prepare_normed_full
        preact = jnp.dot(normed_full, merged, preferred_element_type=jnp.float32)
        sigmoid_pre = jax.nn.sigmoid(preact)
        silu_slope = sigmoid_pre * (1.0 + preact * (1.0 - sigmoid_pre))
        cotangent32 = incoming_cotangent.astype(jnp.float32)
        pre_grad = (cotangent32 * silu_slope).astype(jnp.bfloat16)
        partial_term = lax.dot_general(
            merged, pre_grad, (((1,), (1,)), ((), ())), preferred_element_type=jnp.float32
        )
        norm_grad = (
            lax.psum_scatter(
                lax.optimization_barrier(partial_term.astype(jnp.bfloat16))
                .astype(jnp.float32)
                .astype(jnp.bfloat16),
                "tensor",
                scatter_dimension=0,
                tiled=True,
            )
            .astype(jnp.float32)
            .T
        )
        rowdot = lax.psum(
            jnp.sum(prepare_normed.astype(jnp.float32) * norm_grad, axis=-1), "tensor"
        )
        backward_returned_gradient = (
            cotangent32
            + prepare_rscale * gain_row * norm_grad
            - inputs32 * prepare_rscale * prepare_rscale * rowdot[:, None] / features
        ).astype(jnp.bfloat16)
        gain_term = jnp.sum(norm_grad * inputs32 * prepare_rscale, axis=0)
        returned_gradient, normed_full, pre_grad, gain_term = (
            backward_returned_gradient,
            normed_full,
            pre_grad,
            gain_term,
        )
        normed_list.append(normed_full)
        pregrad_list.append(pre_grad)
        gain_total = gain_total + gain_term
    normed_stack = jnp.concatenate(normed_list, axis=0)
    pregrad_stack = jnp.concatenate(pregrad_list, axis=0)
    grad_w = lax.dot_general(
        normed_stack, pregrad_stack, (((0,), (0,)), ((), ())), preferred_element_type=jnp.float32
    ) / (slot_count * row_count)
    col_inner = jnp.sum(grad_w * direction, axis=0)
    grad_mag = col_inner / colnorm
    dir_grad = (col_scale * (grad_w - direction * (col_inner / (colnorm * colnorm)))).astype(
        jnp.bfloat16
    )
    grad_outproj = jnp.dot(adapter_full, dir_grad, preferred_element_type=jnp.float32)
    column_term = lax.dot_general(
        output_projection[0], dir_grad, (((1,), (1,)), ((), ())), preferred_element_type=jnp.float32
    )
    grad_in = lax.psum_scatter(
        column_term.astype(jnp.bfloat16), "tensor", scatter_dimension=1, tiled=True
    ).astype(jnp.float32)
    gain_grad = gain_total / (slot_count * row_count)
    return (
        emitted_rows[None],
        returned_gradient[None],
        grad_mag[None],
        grad_in[None],
        grad_outproj[None],
        gain_grad[None],
    )


def solution(mesh):
    in_specs = (
        P("section", None, "tensor"),
        P(None, None, "tensor"),
        P("section", None, None, "tensor"),
        P("section", None, "tensor"),
        P(None, None, "tensor"),
        P("section", None, "tensor"),
        P("section", None, "tensor"),
        P("section", None, "tensor"),
        P("section", "tensor"),
        P("section", "tensor"),
    )
    out_specs = (
        P("section", None, "tensor"),
        P("section", None, "tensor"),
        P("section", "tensor"),
        P("section", None, "tensor"),
        P("section", None, "tensor"),
        P("section", "tensor"),
    )
    return jax.shard_map(local, mesh=mesh, in_specs=in_specs, out_specs=out_specs, check_vma=False)
```

profile of v0, /device:TPU:1, one launch (start us, length us, event | category | flops | bytes accessed | tf_op | source)
XLA Modules:
  0.0 394.9 jit_solution(9505584036628855855)
XLA Ops:
  7.2 0.0 copy-start
  7.2 0.0 reduce-scatter.10.cloned.1.call-start
  7.2 0.9 fusion.33
  8.2 29.8 %psum.44 = f32[64]{0:T(128)S(1)} all-reduce(f32[64]{0:T(128)S(1)} %get-tuple-element.9), channel_id=1, replica_groups=mesh['section'=32,'tensor'=16] {'tensor'}, use_global_device_ids=true, to_apply=%region_6.7 | all-reduce | flops 64 | bytes 512 | tf_op jit(solution)/shard_map/psum | solution.py:65
  38.0 0.7 convert_reduce_fusion
  38.7 15.5 %all-gather = bf16[1,16,6144]{2,1,0:T(8,128)(2,1)S(1)} all-gather(bf16[1,16,384]{2,1,0:T(8,128)(2,1)} %param.16), channel_id=2, replica_groups=mesh['section'=32,'tensor'=16] {'tensor'}, dimensions={2}, use_global_device_ids=true | all-gather | bytes 208896 | tf_op jit(solution)/shard_map/all_gather | solution.py:32
  54.1 0.9 fusion.15
  55.0 18.2 %all_gather.18 = bf16[64,6144]{1,0:T(8,128)(2,1)S(1)} all-gather(bf16[64,384]{1,0:T(8,128)(2,1)S(1)} %fusion.15), channel_id=1, replica_groups=mesh['section'=32,'tensor'=16] {'tensor'}, dimensions={1}, use_global_device_ids=true | all-gather | bytes 835584 | tf_op jit(solution)/shard_map/all_gather | solution.py:68
  73.2 0.0 copy-done
  73.2 0.0 copy-start.8
  73.2 4.0 %multiply_reduce_fusion.1 = (f32[384]{0:T(512)S(1)}, f32[6144,384]{1,0:T(8,128)S(1)}) fusion(bf16[1,16,384]{2,1,0:T(8,128)(2,1)S(1)} %copy-done, bf16[1,16,6144]{2,1,0:T(8,128)(2,1)S(1)} %all-gather, bf16[1,6144,384]{2,1,0:T(8,128)(2,1)} %param.15), kind=kOutput, calls=%fused_computation.4 | convolution fusion | flops 84934272 | bytes 14366208 | tf_op jit(solution)/shard_map/rd,rc->dc/dot_general | solution.py:33
  77.2 0.0 copy-start.2
  77.2 0.0 copy-done.8
  77.3 0.9 multiply_convert_fusion.1
  78.2 2.7 copy-done.2
  80.8 0.8 fusion.53
  81.7 1.3 copy-done.1
  83.0 0.0 copy-done.5
  83.0 1.6 convolution_convert_fusion.1
  84.6 1.6 copy.16
  86.2 0.0 reduce-scatter.10.cloned.1.call-update
  86.2 0.0 reduce-scatter.14.cloned.1.call-start
  86.3 0.0 copy-done.4
  86.3 0.1 fusion.26
  86.4 57.5 %reduce-scatter.10.cloned.1.call-done = bf16[384,64]{1,0:T(8,128)(2,1)} async-done(((bf16[6144,64]{1,0:T(8,128)(2,1)}), bf16[384,64]{1,0:T(8,128)(2,1)}) %reduce-scatter.10.cloned.1.call-update) | async-done | bytes 49168
  143.9 1.0 copy.17
  144.9 0.0 copy-done.3
  144.9 0.2 fusion.40
  145.1 25.4 %all-reduce.1 = (f32[64]{0:T(128)S(1)}, f32[64]{0:T(128)S(1)}, f32[64]{0:T(128)S(1)}) all-reduce(f32[64]{0:T(128)S(1)} %fusion.26, f32[64]{0:T(128)S(1)} %fusion.40, f32[64]{0:T(128)S(1)} %get-tuple-element.8), channel_id=1, replica_groups=mesh['section'=32,'tensor'=16] {'tensor'}, use_global_device_ids=true, to_apply=%region_1.0 | all-reduce | flops 192 | bytes 1536 | tf_op jit(solution)/shard_map/psum | solution.py:55
  170.4 0.1 fusion.19
  170.6 1.3 collective-permute-start.1
  171.9 18.4 %all_gather.19 = bf16[64,6144]{1,0:T(8,128)(2,1)S(1)} all-gather(bf16[64,384]{1,0:T(8,128)(2,1)S(1)} %get-tuple-element.21), channel_id=1, replica_groups=mesh['section'=32,'tensor'=16] {'tensor'}, dimensions={1}, use_global_device_ids=true | all-gather | bytes 835584 | tf_op jit(solution)/shard_map/all_gather | solution.py:68
  190.3 0.0 collective-permute-done.1
  190.3 0.0 copy-done.6
  190.3 3.2 fusion.20
  193.5 6.9 %multiply_reduce_fusion = (f32[384]{0:T(512)S(1)}, f32[6144,384]{1,0:T(8,128)}) fusion(f32[6144,384]{1,0:T(8,128)} %copy-done.2, bf16[64,384]{1,0:T(8,128)(2,1)S(1)} %get-tuple-element.16, bf16[64,384]{1,0:T(8,128)(2,1)S(1)} %get-tuple-element.22, bf16[64,6144]{1,0:T(8,128)(2,1)S(1)} %all_gather.19, bf16[64,6144]{1,0:T(8,128)(2,1)S(1)} %all_gather.18), kind=kOutput, calls=%fused_computation.2 | convolution fusion | flops 614399616 | bytes 20547072 | tf_op jit(solution)/shard_map/dot_general | solution.py:111
  200.4 9.8 %multiply_convert_fusion = bf16[6144,384]{1,0:T(8,128)(2,1)} fusion(f32[6144,384]{1,0:T(8,128)} %get-tuple-element.30, f32[6144,384]{1,0:T(8,128)} %copy-done.2, f32[384]{0:T(512)S(1)} %multiply_divide_fusion, f32[384]{0:T(512)S(1)} %multiply_reduce_fusion.2), kind=kLoop, calls=%fused_computation.1 | loop fusion | flops 9437184 | bytes 23596032 | tf_op jit(solution)/shard_map/convert_element_type | solution.py:116
  210.2 3.7 fusion
  213.8 1.5 copy.20
  215.4 0.0 reduce-scatter.14.cloned.1.call-update
  215.4 0.0 reduce-scatter.12.cloned.1.call-start
  215.4 3.9 convolution_convert_fusion
  219.4 0.0 copy-start.7
  219.4 1.6 copy.18
  220.9 0.0 reduce-scatter.12.cloned.1.call-update
  221.0 19.3 %all_gather.15 = bf16[64,6144]{1,0:T(8,128)(2,1)S(1)} all-gather(bf16[64,384]{1,0:T(8,128)(2,1)S(1)} %get-tuple-element.23), channel_id=1, replica_groups=mesh['section'=32,'tensor'=16] {'tensor'}, dimensions={1}, use_global_device_ids=true | all-gather | bytes 835584 | tf_op jit(solution)/shard_map/all_gather | solution.py:59
  240.3 3.2 fusion.29
  243.5 3.8 collective-permute-start
  247.3 0.6 reshape_multiply_fusion
  247.9 0.6 collective-permute-done
  248.5 0.0 copy-done.7
  248.5 0.1 fusion.22
  248.6 3.7 convolution_bitcast_fusion
  252.3 23.7 %reduce-scatter.14.cloned.1.call-done = bf16[384,16]{1,0:T(8,128)(2,1)} async-done(((bf16[6144,16]{1,0:T(8,128)(2,1)}), bf16[384,16]{1,0:T(8,128)(2,1)}) %reduce-scatter.14.cloned.1.call-update) | async-done | bytes 12304
  276.0 1.0 copy.21
  277.0 0.6 bitcast_convert_fusion
  277.6 60.8 %reduce-scatter.12.cloned.1.call-done = bf16[384,64]{1,0:T(8,128)(2,1)} async-done(((bf16[6144,64]{1,0:T(8,128)(2,1)}), bf16[384,64]{1,0:T(8,128)(2,1)}) %reduce-scatter.12.cloned.1.call-update) | async-done | bytes 49168
  338.5 1.0 copy.19
  339.4 0.1 fusion.35
  339.6 0.6 div.77
  340.2 25.3 %all-reduce = (f32[64]{0:T(128)S(1)}, f32[64]{0:T(128)S(1)}) all-reduce(f32[64]{0:T(128)S(1)} %get-tuple-element.18, f32[64]{0:T(128)S(1)} %get-tuple-element.10), channel_id=1, replica_groups=mesh['section'=32,'tensor'=16] {'tensor'}, use_global_device_ids=true, to_apply=%region_4.5 | all-reduce | flops 128 | bytes 1024 | tf_op jit(solution)/shard_map/psum | solution.py:55
  365.5 0.7 fusion.43
  366.2 18.4 %all_gather.17 = bf16[64,6144]{1,0:T(8,128)(2,1)S(1)} all-gather(bf16[64,384]{1,0:T(8,128)(2,1)S(1)} %get-tuple-element.25), channel_id=1, replica_groups=mesh['section'=32,'tensor'=16] {'tensor'}, dimensions={1}, use_global_device_ids=true | all-gather | bytes 835584 | tf_op jit(solution)/shard_map/all_gather | solution.py:59
  384.6 3.8 fusion.47
  (12 shorter events, 0.1 us)
Async XLA Ops:
  7.2 66.0 %copy-start = (bf16[1,16,384]{2,1,0:T(8,128)(2,1)S(1)}, bf16[1,16,384]{2,1,0:T(8,128)(2,1)}, u32[]{:S(2)}) copy-start(bf16[1,16,384]{2,1,0:T(8,128)(2,1)} %param.17) | copy-start | bytes 36868
  7.2 136.7 %reduce-scatter.10.cloned.1.call-start = ((), (), s32[]{:S(2)}) async-start(), calls=%async_computation.3 | async-start | bytes 1671168
  73.2 4.0 %copy-start.8 = (f32[1,384]{1,0:T(1,128)S(1)}, f32[1,384]{1,0:T(1,128)}, u32[]{:S(2)}) copy-start(f32[1,384]{1,0:T(1,128)} %param.18) | copy-start | bytes 4612
  77.2 3.6 copy-start.2
  80.8 2.2 copy-start.1
  80.8 2.2 copy-start.5
  83.0 3.3 copy-start.4
  83.0 61.9 %copy-start.3 = (bf16[1,2,64,384]{3,2,1,0:T(8,128)(2,1)S(1)}, bf16[1,2,64,384]{3,2,1,0:T(8,128)(2,1)}, u32[]{:S(2)}) copy-start(bf16[1,2,64,384]{3,2,1,0:T(8,128)(2,1)} %param.12) | copy-start | bytes 294916
  83.0 107.3 %copy-start.6 = (bf16[1,64,384]{2,1,0:T(8,128)(2,1)S(1)}, bf16[1,64,384]{2,1,0:T(8,128)(2,1)}, u32[]{:S(2)}) copy-start(bf16[1,64,384]{2,1,0:T(8,128)(2,1)} %param.14) | copy-start | bytes 147460
  86.2 189.8 %reduce-scatter.14.cloned.1.call-start = ((), (), s32[]{:S(2)}) async-start(), calls=%async_computation.5 | async-start | bytes 1671168
  170.6 19.7 %collective-permute-start.1 = (bf16[64,384]{1,0:T(8,128)(2,1)S(1)}, bf16[64,384]{1,0:T(8,128)(2,1)S(1)}, u32[]{:S(2)}, u32[]{:S(2)}) collective-permute-start(bf16[64,384]{1,0:T(8,128)(2,1)S(1)} %get-tuple-element.20), channel_id=1, source_target_pairs={{16,0},{32,16},{48,32},{64,48},{80,64},{96,80},{112,96},{128,112},... | collective-permute-start | bytes 147464 | tf_op jit(solution)/shard_map/ppermute | solution.py:10
  215.4 123.1 %reduce-scatter.12.cloned.1.call-start = ((), (), s32[]{:S(2)}) async-start(), calls=%async_computation.4 | async-start | bytes 1671168
  219.4 29.1 %copy-start.7 = (bf16[1,64,384]{2,1,0:T(8,128)(2,1)S(1)}, bf16[1,64,384]{2,1,0:T(8,128)(2,1)}, u32[]{:S(2)}) copy-start(bf16[1,64,384]{2,1,0:T(8,128)(2,1)} %param.11) | copy-start | bytes 147460
  243.5 5.0 %collective-permute-start = (bf16[64,384]{1,0:T(8,128)(2,1)S(1)}, bf16[64,384]{1,0:T(8,128)(2,1)S(1)}, u32[]{:S(2)}, u32[]{:S(2)}) collective-permute-start(bf16[64,384]{1,0:T(8,128)(2,1)S(1)} %fusion.29), channel_id=1, source_target_pairs={{0,16},{16,32},{32,48},{48,64},{64,80},{80,96},{96,112},{112,128},... | collective-permute-start | bytes 147464 | tf_op jit(solution)/shard_map/ppermute | solution.py:10
Sparse Core Ops, SparseCore 0:
  86.3 57.5 reduce-scatter.9
  215.5 60.4 reduce-scatter.13
  278.9 59.5 reduce-scatter.11
where the time goes:
time: 396 us; the launch traced here: 395 us
  blocking collectives  170 us (43%)
  waiting for transfers between devices  143 us (36%)
  matrix products  34.8 us (9%)
  other arithmetic  15.9 us (4%)
  between operations  13.9 us (4%)
  local copies, waits for them, and re-layouts  12.1 us (3%)
  starting transfers between devices  5.24 us (1%)
    unnamed x6, waiting for transfers between devices  142 us
    psum x2, blocking collectives, local(): lax.psum(jnp.sum(forward_inputs32 * forward_inputs32, axis=-1), 'tensor')  50.7 us
    all_gather x2, blocking collectives, local(): lax.all_gather(forward_normed, 'tensor', axis=1, tiled=True)  37.7 us
    all_gather x2, blocking collectives, local(): lax.all_gather(prepare_normed, 'tensor', axis=1, tiled=True)  36.6 us
    psum x1, blocking collectives, local(): lax.psum(jnp.sum(prepare_inputs32 * prepare_inputs32, axis=-1), 'tensor')  29.8 us
    all_gather x1, blocking collectives, local(): lax.all_gather(input_projection[0], 'tensor', axis=1, tiled=True)  15.5 us
    unnamed x24, local copies, waits for them, and re-layouts  11.6 us
    convert_element_type x1, other arithmetic, local(): (col_scale * (grad_w - direction * (col_inner / (colnorm * colnorm)))).as...  9.83 us
  transfers between devices with their start and end apart: 5, of which 4 were waited for; matrix products, arithmetic and copies ran while one was open for 4% of the time, Pallas kernels for 0%

commit v1 on v0

v1 whole, which is shorter than its diff:
```python
import jax
import jax.numpy as jnp
from jax import lax
from jax.experimental import pallas as pl
from jax.experimental.pallas import tpu as pltpu
from jax.sharding import PartitionSpec as P

F32 = jnp.float32
BF16 = jnp.bfloat16
CHIPS = 8
TOK = 64
RANK = 16
COLS = 384
PAIR = 2 * COLS
FEATURES = CHIPS * PAIR
SLOTS = 2
ORDER = (3, 5, 4, 1, 7, 2, 6, 0)
COPIES = 160


def dot(a, b):
    return jnp.dot(a, b, preferred_element_type=F32)


def dot_nt(a, b):
    return lax.dot_general(a, b, (((1,), (1,)), ((), ())), preferred_element_type=F32)


def dot_tn(a, b):
    return lax.dot_general(a, b, (((0,), (0,)), ((), ())), preferred_element_type=F32)


def lane_groups(x):
    total = x[:, 0:128]
    for start in range(128, x.shape[1], 128):
        total = total + x[:, start : start + 128]
    return total


def row_to_column(row):
    square = jnp.transpose(jnp.broadcast_to(row, (128, 128)))
    return square[0:TOK, 0:1]


def column_partials_to_row(partials):
    padded = jnp.concatenate([partials, jnp.zeros((128 - TOK, 128), F32)], axis=0)
    return jnp.sum(jnp.transpose(padded), axis=0, keepdims=True)


def kernel(
    act_hbm, ent_hbm, sta_hbm, tg_hbm, ret_hbm, frozen_hbm, ain_hbm, aout_hbm, mag_ref, gain_ref,
    act_o, grad_o, mag_o, gin_o, gout_o, gain_o,
    fz, w, g0, g1, g2, g3, gn, zn0, zn1, tg, ent, ret, aout, em, x1, gr, gx,
    pb0, sb0, sv0, rv0, pb1, sb1, sv1, rv1, rd0, rd1, ssem, rsem, lsem,
):
    me = lax.axis_index("tensor")
    sec = lax.axis_index("section")
    sections = lax.axis_size("section")
    y = me // 2
    core = me - 2 * y
    mine = pl.ds(pl.multiple_of(core * COLS, 128), COLS)
    other = pl.ds(pl.multiple_of((1 - core) * COLS, 128), COLS)

    def chip(offset):
        return {"tensor": lax.rem(y + offset + CHIPS, CHIPS) * 2 + core}

    sibling = {"tensor": me + 1 - 2 * core}
    after = {"section": lax.rem(sec + 1, sections)}
    before = {"section": lax.rem(sec + sections - 1, sections)}

    counter = [0]
    started = []

    def send(src, dst, device):
        index = counter[0]
        counter[0] += 1
        copy = pltpu.make_async_remote_copy(
            src_ref=src, dst_ref=dst, send_sem=ssem.at[index], recv_sem=rsem.at[index],
            device_id=device, device_id_type=MESH,
        )
        copy.start()
        started.append(copy)
        return copy

    locals_ = []

    def load(src, dst):
        copy = pltpu.make_async_copy(src, dst, lsem.at[len(locals_)])
        copy.start()
        locals_.append(copy)
        return copy

    l_s0 = load(sta_hbm.at[0, 0], g0.at[0, 0:TOK, mine])
    l_a = load(ain_hbm.at[0], g0.at[0, TOK : TOK + RANK, mine])
    l_fz = load(frozen_hbm.at[0], fz)
    l_p = load(aout_hbm.at[0], aout)
    l_t0 = load(act_hbm.at[0], g1.at[0, :, mine])
    l_tg = load(tg_hbm.at[0], tg)
    l_s1 = load(sta_hbm.at[0, 1], g2.at[0, :, mine])
    l_ent = load(ent_hbm.at[0], ent)
    l_ret = load(ret_hbm.at[0], ret)

    barrier = pltpu.get_barrier_semaphore()
    peers = [chip(1), chip(-1), chip(2), chip(-2), sibling, after, before]
    for peer in peers:
        pl.semaphore_signal(barrier, inc=1, device_id=peer, device_id_type=MESH)
    gain = gain_ref[...].astype(F32)
    gn[0, 0:1, mine] = gain
    pl.semaphore_wait(barrier, len(peers))

    class Gather:
        def __init__(self, ref, rows, split, lead=None):
            self.parts = [(ref, slice(0, rows), split)]
            if lead is not None:
                self.parts = [(lead, slice(0, 1), None)] + self.parts
            self.near = {}
            self.far = {}
            self.sib = {}

        def begin(self):
            for offset in (2, -2, 1, -1):
                slot = (-offset) % CHIPS
                for n, (ref, rows, _) in enumerate(self.parts):
                    self.near[slot, n] = send(ref.at[0, rows, mine], ref.at[slot, rows, mine], chip(offset))
                if offset == 2:
                    self.share(0)

        def share(self, slot):
            for n, (ref, rows, _) in enumerate(self.parts):
                self.sib[slot, n] = send(ref.at[slot, rows, mine], ref.at[slot, rows, mine], sibling)

        def pass_on(self):
            for held, step, low in ((6, 1, True), (2, -1, False)):
                for n, (ref, rows, split) in enumerate(self.parts):
                    self.near[held, n].wait_recv()
                    slot = (held - step) % CHIPS
                    self.far[slot, n] = [send(ref.at[held, rows, mine], ref.at[slot, rows, mine], chip(step))]
                    if split is None:
                        if low:
                            self.far[4, n] = [send(ref.at[held, rows, mine], ref.at[4, rows, mine], chip(2))]
                    else:
                        part = slice(0, split) if low else slice(split, rows.stop)
                        self.far.setdefault((4, n), []).append(
                            send(ref.at[held, part, mine], ref.at[4, part, mine], chip(2 * step))
                        )
                self.share(held)

        def share_near(self):
            for slot in (7, 1):
                for n in range(len(self.parts)):
                    self.near[slot, n].wait_recv()
                self.share(slot)

        def share_far(self):
            for slot in (5, 3, 4):
                for n in range(len(self.parts)):
                    for copy in self.far[slot, n]:
                        copy.wait_recv()
                self.share(slot)

        def ready(self, slot):
            for n in range(len(self.parts)):
                self.sib[slot, n].wait_recv()

    def base_of(slot):
        return pl.multiple_of(lax.rem(y + slot, CHIPS) * PAIR, PAIR)

    def build(slot, norms):
        base = base_of(slot)
        for part in range(3):
            lanes = slice(part * 256, (part + 1) * 256)
            rows = pl.ds(pl.multiple_of(base + part * 256, 256), 256)
            direction = fz[rows, :].astype(F32) + dot_tn(g0[slot, TOK : TOK + RANK, lanes], aout[...])
            w[rows, :] = direction.astype(BF16)
            norms = norms + jnp.sum((direction * direction).reshape(32, 8, COLS), axis=0)
        return norms

    def chunk(ref, slot, squares, total, with_adapter=False):
        z = ref[slot, 0:TOK, :].astype(F32)
        squares = squares + lane_groups(z * z)
        scaled = (z * gn[slot, 0:1, :]).astype(BF16)
        if with_adapter:
            scaled = jnp.concatenate([scaled, ref[slot, TOK : TOK + RANK, :]], axis=0)
        total = total + dot(scaled, w[pl.ds(base_of(slot), PAIR), :])
        return squares, total

    def rscale_of(squares):
        return lax.rsqrt(jnp.sum(squares, axis=1, keepdims=True) / FEATURES + 1e-05)

    def normalise(ref, out, rscale):
        for slot in range(CHIPS):
            z = ref[slot, 0:TOK, :].astype(F32)
            out[slot] = (z * rscale * gn[slot, 0:1, :]).astype(BF16)

    def slope_of(preact):
        sig = 1.0 / (1.0 + jnp.exp(-preact))
        return sig * (1.0 + preact * (1.0 - sig))

    class Scatter:
        def __init__(self, rows, split, pb, sb, sv, rv, rd):
            self.rows, self.split = rows, split
            self.pb, self.sb, self.sv, self.rv, self.rd = pb, sb, sv, rv, rd

        def compute(self, lhs, dots, extra=None):
            self.rd[0] = jnp.broadcast_to(dots, (8, 128))
            self.rd_sib = send(self.rd.at[0], self.rd.at[1], sibling)
            for n, slot in enumerate(ORDER):
                value = dot_nt(lhs, w[pl.ds(base_of(slot), PAIR), :])
                if extra is not None:
                    value = jnp.concatenate([value[0:TOK], value[TOK:] + extra(slot)], axis=0)
                self.pb[n] = value.astype(BF16)
                if n == 2:
                    self.first = send(self.pb.at[0:3, :, other], self.sb.at[0:3], sibling)
            self.second = send(self.pb.at[3:8, :, other], self.sb.at[3:8], sibling)

        def pair_sum(self, n):
            return self.pb[n, :, mine].astype(F32) + self.sb[n].astype(F32)

        def stage_one(self):
            rd, rv, sv = self.rd, self.rv, self.sv
            self.first.wait_recv()
            sv[2] = self.pair_sum(2).astype(BF16)
            low, high = slice(0, self.split), slice(self.split, self.rows)
            self.r4a = send(sv.at[2, low], rv.at[2, low], chip(-2))
            self.r4b = send(sv.at[2, high], rv.at[2, high], chip(2))
            sv[0] = self.pair_sum(0).astype(BF16)
            self.r1 = send(sv.at[0], rv.at[0], chip(1))
            sv[1] = self.pair_sum(1).astype(BF16)
            self.r2 = send(sv.at[1], rv.at[1], chip(-1))
            self.rd_sib.wait_recv()
            rd[2] = rd[0] + rd[1]
            self.rd_a = send(rd.at[2], rd.at[3], chip(1))
            self.rd_b = send(rd.at[2], rd.at[4], chip(-1))
            self.rd_c = send(rd.at[2], rd.at[5], chip(-2))

        def stage_one_direct(self):
            rv, sv = self.rv, self.sv
            self.second.wait_recv()
            sv[3] = self.pair_sum(3).astype(BF16)
            self.d1 = send(sv.at[3], rv.at[3], chip(1))
            sv[4] = self.pair_sum(4).astype(BF16)
            self.d2 = send(sv.at[4], rv.at[4], chip(-1))

        def stage_two(self):
            rv, sv, rd = self.rv, self.sv, self.rd
            split = self.split
            self.r1.wait_recv()
            self.r4b.wait_recv()
            total = self.pair_sum(5) + rv[0].astype(F32)
            total = jnp.concatenate([total[0:split], total[split:] + rv[2, split:].astype(F32)], axis=0)
            sv[5] = total.astype(BF16)
            self.e1 = send(sv.at[5], rv.at[5], chip(2))
            self.r2.wait_recv()
            self.r4a.wait_recv()
            total = self.pair_sum(6) + rv[1].astype(F32)
            total = jnp.concatenate([total[0:split] + rv[2, 0:split].astype(F32), total[split:]], axis=0)
            sv[6] = total.astype(BF16)
            self.e2 = send(sv.at[6], rv.at[6], chip(-2))
            self.rd_a.wait_recv()
            self.rd_b.wait_recv()
            self.rd_c.wait_recv()
            rd[6] = rd[2] + rd[3]
            self.rd_e = send(rd.at[6], rd.at[8], chip(2))
            rd[7] = rd[2] + rd[4] + rd[5]
            self.rd_f = send(rd.at[7], rd.at[9], chip(-2))

        def final(self):
            rv, rd = self.rv, self.rd
            total = self.pair_sum(7)
            self.d1.wait_recv()
            self.d2.wait_recv()
            total = total + rv[3].astype(F32) + rv[4].astype(F32)
            self.rd_e.wait_recv()
            self.rd_f.wait_recv()
            dots = rd[2] + rd[3] + rd[4] + rd[8] + rd[9]
            self.e1.wait_recv()
            self.e2.wait_recv()
            total = total + rv[5].astype(F32) + rv[6].astype(F32)
            return total, row_to_column(dots[0:1, :])

    ga_s0 = Gather(g0, TOK + RANK, 48, lead=gn)
    ga_t0 = Gather(g1, TOK, 32)
    ga_s1 = Gather(g2, TOK, 32)
    ga_t1 = Gather(g3, TOK, 32)
    rs0 = Scatter(TOK, 32, pb0, sb0, sv0, rv0, rd0)
    rs1 = Scatter(TOK + RANK, 48, pb1, sb1, sv1, rv1, rd1)

    def fresh():
        return jnp.zeros((TOK, 128), F32), jnp.zeros((TOK, COLS), F32)

    l_s0.wait()
    l_a.wait()
    ga_s0.begin()
    l_fz.wait()
    l_p.wait()
    norms = jnp.zeros((8, COLS), F32)
    squares = jnp.zeros((TOK, 128), F32)
    total = jnp.zeros((TOK + RANK, COLS), F32)
    ga_s0.ready(0)
    norms = build(0, norms)
    squares, total = chunk(g0, 0, squares, total, True)
    ga_s0.pass_on()
    l_t0.wait()
    ga_t0.begin()
    ga_s0.share_near()
    for slot in (6, 2, 7, 1):
        ga_s0.ready(slot)
        norms = build(slot, norms)
        squares, total = chunk(g0, slot, squares, total, True)
    ga_s0.share_far()
    for slot in (5, 3, 4):
        ga_s0.ready(slot)
        norms = build(slot, norms)
        squares, total = chunk(g0, slot, squares, total, True)
    norm_squares = jnp.sum(norms, axis=0, keepdims=True) + 1e-06
    colnorm = jnp.sqrt(norm_squares)
    col_scale = mag_ref[...] / colnorm
    r0 = rscale_of(squares)
    raw0 = total[0:TOK] * r0
    adapter_direction = total[TOK:]
    preact = raw0 * col_scale
    l_tg.wait()
    cot0 = tg[...].astype(F32)
    pg = cot0 * slope_of(preact)
    pgs0 = (pg * col_scale).astype(BF16)
    inner = jnp.sum(pg * raw0, axis=0, keepdims=True)
    rs0.compute(pgs0, column_partials_to_row(lane_groups(pg * preact)))
    ga_t0.pass_on()
    l_s1.wait()
    rs0.stage_one()
    ga_s1.begin()
    rs0.stage_one_direct()
    ga_t0.share_near()
    squares, total = fresh()
    for slot in (0, 6, 2, 7, 1):
        ga_t0.ready(slot)
        squares, total = chunk(g1, slot, squares, total)
    rs0.stage_two()
    ga_t0.share_far()
    for slot in (5, 3, 4):
        ga_t0.ready(slot)
        squares, total = chunk(g1, slot, squares, total)
    preact = total * rscale_of(squares) * col_scale
    emitted = g1[0, :, mine].astype(F32) + preact / (1.0 + jnp.exp(-preact))
    l_ent.wait()
    em[...] = jnp.where(sec == sections - 1, ent[...], emitted.astype(BF16))
    shift_act = send(em, g3.at[0, :, mine], after)
    ga_s1.pass_on()
    normalise(g0, zn0, r0)
    norm_grad, rowdot = rs0.final()
    own = g0[0, 0:TOK, mine].astype(F32)
    returned = cot0 + r0 * gain * norm_grad - own * (r0 * r0 * rowdot / FEATURES)
    l_ret.wait()
    gr[...] = jnp.where(sec == 0, ret[...], returned.astype(BF16))
    shift_cot = send(gr, gx, before)
    gain_total = jnp.sum(norm_grad * own * r0, axis=0, keepdims=True)
    ga_s1.share_near()
    shift_act.wait_recv()
    ga_t1.begin()
    squares, total = fresh()
    for slot in (0, 6, 2, 7, 1):
        ga_s1.ready(slot)
        squares, total = chunk(g2, slot, squares, total)
    ga_s1.share_far()
    for slot in (5, 3, 4):
        ga_s1.ready(slot)
        squares, total = chunk(g2, slot, squares, total)
    r1 = rscale_of(squares)
    raw1 = total * r1
    preact = raw1 * col_scale
    slope = slope_of(preact)
    normalise(g2, zn1, r1)
    factor = aout[...]
    mean = 1.0 / (SLOTS * TOK)
    weights0 = dot_nt(factor, pgs0)
    shift_cot.wait_recv()
    cot1 = gx[...].astype(F32)
    pg = cot1 * slope
    pgs1 = (pg * col_scale).astype(BF16)
    inner = (inner + jnp.sum(pg * raw1, axis=0, keepdims=True)) * mean
    ratio = inner / norm_squares
    scaled_ratio = col_scale * ratio
    weights = (jnp.concatenate([weights0, dot_nt(factor, pgs1)], axis=1) * mean).astype(BF16)
    shrunk = (factor.astype(F32) * -scaled_ratio).astype(BF16)

    def column_extra(slot):
        return dot(weights, jnp.concatenate([zn0[slot], zn1[slot]], axis=0))

    rs1.compute(
        jnp.concatenate([pgs1, shrunk], axis=0),
        column_partials_to_row(lane_groups(pg * preact)),
        column_extra,
    )
    rs1.stage_one()
    ga_t1.pass_on()
    rs1.stage_one_direct()
    ga_t1.share_near()
    mag_o[...] = inner / colnorm
    product = jnp.zeros((RANK, TOK * SLOTS), F32)
    for slot in range(CHIPS):
        product = product + dot_nt(
            g0[slot, TOK : TOK + RANK, :], jnp.concatenate([zn0[slot], zn1[slot]], axis=0)
        )
    upper = product.astype(BF16)
    lower = (product - upper.astype(F32)).astype(BF16)
    both = dot(jnp.concatenate([upper, lower], axis=0), jnp.concatenate([pgs0, pgs1], axis=0))
    gout_o[0] = (both[0:RANK] + both[RANK:]) * mean - adapter_direction * scaled_ratio
    rs1.stage_two()
    squares, total = fresh()
    for slot in (0, 6, 2, 7, 1):
        ga_t1.ready(slot)
        squares, total = chunk(g3, slot, squares, total)
    ga_t1.share_far()
    for slot in (5, 3, 4):
        ga_t1.ready(slot)
        squares, total = chunk(g3, slot, squares, total)
    preact = total * rscale_of(squares) * col_scale
    act_o[0] = (g3[0, :, mine].astype(F32) + preact / (1.0 + jnp.exp(-preact))).astype(BF16)
    norm_grad, rowdot = rs1.final()
    gin_o[0] = norm_grad[TOK:]
    norm_grad = norm_grad[0:TOK]
    own = g2[0, :, mine].astype(F32)
    grad_o[0] = (cot1 + r1 * gain * norm_grad - own * (r1 * r1 * rowdot / FEATURES)).astype(BF16)
    gain_total = gain_total + jnp.sum(norm_grad * own * r1, axis=0, keepdims=True)
    gain_o[...] = gain_total * mean
    for copy in started:
        copy.wait_send()


MESH = pl.DeviceIdType.MESH


def local(*args):
    anywhere = pl.BlockSpec(memory_space=pl.ANY)
    vmem = pl.BlockSpec(memory_space=pltpu.VMEM)
    rows1 = TOK + RANK

    def scatter_buffers(rows):
        return [
            pltpu.VMEM((8, rows, PAIR), BF16),
            pltpu.VMEM((8, rows, COLS), BF16),
            pltpu.VMEM((7, rows, COLS), BF16),
            pltpu.VMEM((7, rows, COLS), BF16),
        ]

    gathered = pltpu.VMEM((CHIPS, TOK, PAIR), BF16)
    block = pltpu.VMEM((TOK, COLS), BF16)
    return pl.pallas_call(
        kernel,
        out_shape=(
            jax.ShapeDtypeStruct((1, TOK, COLS), BF16),
            jax.ShapeDtypeStruct((1, TOK, COLS), BF16),
            jax.ShapeDtypeStruct((1, COLS), F32),
            jax.ShapeDtypeStruct((1, RANK, COLS), F32),
            jax.ShapeDtypeStruct((1, RANK, COLS), F32),
            jax.ShapeDtypeStruct((1, COLS), F32),
        ),
        in_specs=[anywhere] * 8 + [vmem] * 2,
        out_specs=(vmem,) * 6,
        scratch_shapes=[
            pltpu.VMEM((FEATURES, COLS), BF16),
            pltpu.VMEM((FEATURES, COLS), BF16),
            pltpu.VMEM((CHIPS, rows1, PAIR), BF16),
            gathered,
            gathered,
            gathered,
            pltpu.VMEM((CHIPS, 8, PAIR), F32),
            gathered,
            gathered,
            block,
            block,
            block,
            pltpu.VMEM((RANK, COLS), BF16),
            block,
            block,
            block,
            block,
            *scatter_buffers(TOK),
            *scatter_buffers(rows1),
            pltpu.VMEM((10, 8, 128), F32),
            pltpu.VMEM((10, 8, 128), F32),
            pltpu.SemaphoreType.DMA((COPIES,)),
            pltpu.SemaphoreType.DMA((COPIES,)),
            pltpu.SemaphoreType.DMA((9,)),
        ],
        compiler_params=pltpu.CompilerParams(
            collective_id=0, has_side_effects=True, vmem_limit_bytes=44 * 2**20
        ),
        name="window",
    )(*args)


def solution(mesh):
    in_specs = (
        P("section", None, "tensor"),
        P(None, None, "tensor"),
        P("section", None, None, "tensor"),
        P("section", None, "tensor"),
        P(None, None, "tensor"),
        P("section", None, "tensor"),
        P("section", None, "tensor"),
        P("section", None, "tensor"),
        P("section", "tensor"),
        P("section", "tensor"),
    )
    out_specs = (
        P("section", None, "tensor"),
        P("section", None, "tensor"),
        P("section", "tensor"),
        P("section", None, "tensor"),
        P("section", None, "tensor"),
        P("section", "tensor"),
    )
    return jax.shard_map(local, mesh=mesh, in_specs=in_specs, out_specs=out_specs, check_vma=False)
```

time: 396 us -> 80.1 us (0.20)
  blocking collectives: 170 us -> 0 us
  waiting for transfers between devices: 143 us -> 0 us
  Pallas kernels: 0 us -> 66.1 us
  matrix products: 34.8 us -> 0 us
  other arithmetic: 15.9 us -> 0 us
  between operations: 13.9 us -> 0.66 us
  starting transfers between devices: 5.24 us -> 0 us
    unnamed x6 -> x0, waiting for transfers between devices: 142 us -> none
    all_gather x5 -> x0, blocking collectives: 89.7 us -> none  [the longest x2 37.7 us: local(): lax.all_gather(forward_normed, 'tensor', axis=1, tiled=True)]
    psum x3 -> x0, blocking collectives: 80.4 us -> none  [the longest x2 50.7 us: local(): lax.psum(jnp.sum(forward_inputs32 * forward_inputs32, axis=-1), 'tensor')]
    pallas_call x0 -> x1, Pallas kernels: none -> 66.1 us  [local(): pl.pallas_call(kernel, out_shape=(jax.ShapeDtypeStruct((1, TOK, COLS), BF...]
    dot_general x10 -> x0, matrix products: 34.8 us -> none  [the longest x2 7.01 us: local(): jnp.dot(lax.all_gather(forward_normed, 'tensor', axis=1, tiled=True), mer...]
    convert_element_type x4 -> x0, other arithmetic: 11.7 us -> none  [the longest x1 9.83 us: local(): (col_scale * (grad_w - direction * (col_inner / (colnorm * colnorm)))).as...]
    ppermute x2 -> x0, starting transfers between devices: 5.12 us -> none  [shifted(): return lax.ppermute(block, axis, route)]
    unnamed x24 -> x26, local copies, waits for them, and re-layouts: 11.6 us -> 12.8 us
  transfers between devices with their start and end apart: 5 -> 0, of which waited for: 4 -> 0; matrix products, arithmetic and copies ran while one was open for 4% -> 0% of each run, Pallas kernels for 0% -> 0%
where the time goes in v1:
time: 80.1 us; the launch traced here: 79.6 us
  Pallas kernels  66.1 us (83%)
  local copies, waits for them, and re-layouts  12.8 us (16%)
    pallas_call x1, Pallas kernels, local(): pl.pallas_call(kernel, out_shape=(jax.ShapeDtypeStruct((1, TOK, COLS), BF...  66.1 us
    unnamed x26, local copies, waits for them, and re-layouts  12.8 us

profile of v1, /device:TPU:1, one launch (start us, length us, event | category | flops | bytes accessed | tf_op | source)
XLA Modules:
  0.0 79.6 jit_solution(5455486725119976363)
XLA Ops:
  0.6 0.0 copy-start
  0.6 2.3 %copy-done = bf16[1,6144,384]{2,1,0:T(8,128)(2,1)S(1)} copy-done((bf16[1,6144,384]{2,1,0:T(8,128)(2,1)S(1)}, bf16[1,6144,384]{2,1,0:T(8,128)(2,1)}, u32[]{:S(2)}) %copy-start) | copy-done | bytes 4718616
  3.0 0.0 copy-start.1
  3.0 0.9 %copy-done.1 = bf16[1,2,64,384]{3,2,1,0:T(8,128)(2,1)S(1)} copy-done((bf16[1,2,64,384]{3,2,1,0:T(8,128)(2,1)S(1)}, bf16[1,2,64,384]{3,2,1,0:T(8,128)(2,1)}, u32[]{:S(2)}) %copy-start.1) | copy-done | bytes 98328
  3.9 0.0 copy-start.2
  3.9 0.8 %copy-done.2 = bf16[1,64,384]{2,1,0:T(8,128)(2,1)S(1)} copy-done((bf16[1,64,384]{2,1,0:T(8,128)(2,1)S(1)}, bf16[1,64,384]{2,1,0:T(8,128)(2,1)}, u32[]{:S(2)}) %copy-start.2) | copy-done | bytes 49176
  4.7 0.0 copy-start.3
  4.7 0.8 %copy-done.3 = bf16[1,64,384]{2,1,0:T(8,128)(2,1)S(1)} copy-done((bf16[1,64,384]{2,1,0:T(8,128)(2,1)S(1)}, bf16[1,64,384]{2,1,0:T(8,128)(2,1)}, u32[]{:S(2)}) %copy-start.3) | copy-done | bytes 49176
  5.5 0.0 copy-start.4
  5.5 0.8 %copy-done.4 = bf16[1,64,384]{2,1,0:T(8,128)(2,1)S(1)} copy-done((bf16[1,64,384]{2,1,0:T(8,128)(2,1)S(1)}, bf16[1,64,384]{2,1,0:T(8,128)(2,1)}, u32[]{:S(2)}) %copy-start.4) | copy-done | bytes 49176
  6.3 0.0 copy-start.5
  6.3 0.8 %copy-done.5 = bf16[1,64,384]{2,1,0:T(8,128)(2,1)S(1)} copy-done((bf16[1,64,384]{2,1,0:T(8,128)(2,1)S(1)}, bf16[1,64,384]{2,1,0:T(8,128)(2,1)}, u32[]{:S(2)}) %copy-start.5) | copy-done | bytes 49176
  7.1 0.0 copy-start.6
  7.1 0.7 copy-done.6
  7.8 0.0 copy-start.7
  7.8 0.7 copy-done.7
  8.5 0.0 copy-start.8
  8.5 0.7 copy-done.8
  9.2 0.0 copy-start.9
  9.2 0.7 copy-done.9
  9.8 66.1 %window.1 = (bf16[1,64,384]{2,1,0:T(8,128)(2,1)S(1)}, bf16[1,64,384]{2,1,0:T(8,128)(2,1)S(1)}, f32[1,384]{1,0:T(1,128)S(1)}, f32[1,16,384]{2,1,0:T(8,128)S(1)}, ...) custom-call(bf16[1,64,384]{2,1,0:T(8,128)(2,1)S(1)} %copy-done.2, bf16[1,64,384]{2,1,0:T(8,128)(2,1)S(1)} %copy-done.3, ...), custom_call_target="tpu_custom_call" | custom-call | tf_op jit(solution)/shard_map/window/pallas_call | solution.py:448
  76.0 0.6 copy.22
  76.6 0.6 copy.23
  77.2 0.6 copy.24
  77.8 0.6 copy.25
  78.4 0.6 copy.26
  79.0 0.6 copy.27
Async XLA Ops:
  0.6 2.3 %copy-start = (bf16[1,6144,384]{2,1,0:T(8,128)(2,1)S(1)}, bf16[1,6144,384]{2,1,0:T(8,128)(2,1)}, u32[]{:S(2)}) copy-start(bf16[1,6144,384]{2,1,0:T(8,128)(2,1)} %frozen_hbm.1) | copy-start | bytes 14155780
  3.0 0.9 %copy-start.1 = (bf16[1,2,64,384]{3,2,1,0:T(8,128)(2,1)S(1)}, bf16[1,2,64,384]{3,2,1,0:T(8,128)(2,1)}, u32[]{:S(2)}) copy-start(bf16[1,2,64,384]{3,2,1,0:T(8,128)(2,1)} %sta_hbm.1) | copy-start | bytes 294916
  3.9 0.8 %copy-start.2 = (bf16[1,64,384]{2,1,0:T(8,128)(2,1)S(1)}, bf16[1,64,384]{2,1,0:T(8,128)(2,1)}, u32[]{:S(2)}) copy-start(bf16[1,64,384]{2,1,0:T(8,128)(2,1)} %act_hbm.1) | copy-start | bytes 147460
  4.7 0.8 %copy-start.3 = (bf16[1,64,384]{2,1,0:T(8,128)(2,1)S(1)}, bf16[1,64,384]{2,1,0:T(8,128)(2,1)}, u32[]{:S(2)}) copy-start(bf16[1,64,384]{2,1,0:T(8,128)(2,1)} %ent_hbm.1) | copy-start | bytes 147460
  5.5 0.8 %copy-start.4 = (bf16[1,64,384]{2,1,0:T(8,128)(2,1)S(1)}, bf16[1,64,384]{2,1,0:T(8,128)(2,1)}, u32[]{:S(2)}) copy-start(bf16[1,64,384]{2,1,0:T(8,128)(2,1)} %tg_hbm.1) | copy-start | bytes 147460
  6.3 0.8 %copy-start.5 = (bf16[1,64,384]{2,1,0:T(8,128)(2,1)S(1)}, bf16[1,64,384]{2,1,0:T(8,128)(2,1)}, u32[]{:S(2)}) copy-start(bf16[1,64,384]{2,1,0:T(8,128)(2,1)} %ret_hbm.1) | copy-start | bytes 147460
  7.1 0.7 copy-start.6
  7.8 0.7 copy-start.7
  8.5 0.7 copy-start.8
  9.2 0.7 copy-start.9

commit v2 on v1

v2 whole, which is shorter than its diff:
```python
import jax
import jax.numpy as jnp
from jax import lax
from jax.experimental import pallas as pl
from jax.experimental.pallas import tpu as pltpu
from jax.sharding import PartitionSpec as P

F32 = jnp.float32
BF16 = jnp.bfloat16
MESH = pl.DeviceIdType.MESH
CHIPS = 8
TOK = 64
RANK = 16
COLS = 384
PAIR = 2 * COLS
FEATURES = CHIPS * PAIR
SLOTS = 2
ORDER = (3, 5, 4, 1, 7, 2, 6, 0)
COPIES = 160


def dot(a, b):
    return jnp.dot(a, b, preferred_element_type=F32)


def dot_nt(a, b):
    return lax.dot_general(a, b, (((1,), (1,)), ((), ())), preferred_element_type=F32)


def dot_tn(a, b):
    return lax.dot_general(a, b, (((0,), (0,)), ((), ())), preferred_element_type=F32)


def lane_groups(x):
    total = x[:, 0:128]
    for start in range(128, x.shape[1], 128):
        total = total + x[:, start : start + 128]
    return total


def kernel(
    act_hbm, ent_hbm, sta_hbm, tg_hbm, ret_hbm, frozen_hbm, ain_hbm, aout_hbm, mag_ref, gain_ref,
    act_o, grad_o, mag_o, gin_o, gout_o, gain_o,
    fz, w, g0, g1, g2, g3, gn, zn0, zn1, tg, tgx, ent, ret, aout, em, gx,
    pb0, sb0, sv0, rv0, pb1, sb1, sv1, rv1, gt, gts, gtv, gtr, ssem, rsem, lsem,
):
    me = lax.axis_index("tensor")
    sec = lax.axis_index("section")
    sections = lax.axis_size("section")
    y = me // 2
    core = me - 2 * y
    mine = pl.ds(pl.multiple_of(core * COLS, 128), COLS)
    other = pl.ds(pl.multiple_of((1 - core) * COLS, 128), COLS)

    def chip(offset):
        return {"tensor": lax.rem(y + offset + CHIPS, CHIPS) * 2 + core}

    def previous(offset):
        return {"section": sec - 1, **chip(offset)}

    def following(offset):
        return {"section": sec + 1, **chip(offset)}

    sibling = {"tensor": me + 1 - 2 * core}
    has_previous = sec > 0
    has_following = sec < sections - 1
    no_previous = jnp.logical_not(has_previous)

    counter = [0]
    started = []

    def send(src, dst, device, condition=None, arrival=None):
        index = counter[0]
        counter[0] += 1
        arrival = index if arrival is None else arrival
        copy = pltpu.make_async_remote_copy(
            src_ref=src, dst_ref=dst, send_sem=ssem.at[index], recv_sem=rsem.at[arrival],
            device_id=device, device_id_type=MESH,
        )
        if condition is None:
            copy.start()
        else:
            pl.when(condition)(copy.start)
        started.append((copy, condition))
        return copy

    locals_ = []

    def load(src, dst):
        copy = pltpu.make_async_copy(src, dst, lsem.at[len(locals_)])
        copy.start()
        locals_.append(copy)
        return copy

    l_s0 = load(sta_hbm.at[0, 0], g0.at[0, 0:TOK, mine])
    l_a = load(ain_hbm.at[0], g0.at[0, TOK : TOK + RANK, mine])
    l_fz = load(frozen_hbm.at[0], fz)
    l_p = load(aout_hbm.at[0], aout)
    l_t0 = load(act_hbm.at[0], g1.at[0, :, mine])
    l_tg = load(tg_hbm.at[0], tg)
    l_s1 = load(sta_hbm.at[0, 1], g2.at[0, :, mine])
    l_ent = load(ent_hbm.at[0], ent)
    l_ret = load(ret_hbm.at[0], ret)

    barrier = pltpu.get_barrier_semaphore()
    near = (0, 1, -1, 2, -2)

    def greet(peers):
        for peer in peers:
            pl.semaphore_signal(barrier, inc=1, device_id=peer, device_id_type=MESH)

    greet([chip(offset) for offset in near[1:]] + [sibling])

    @pl.when(has_previous)
    def _():
        greet([previous(offset) for offset in near])

    @pl.when(has_following)
    def _():
        greet([following(offset) for offset in near])

    gain = gain_ref[...].astype(F32)
    gn[0, 0:1, mine] = gain
    expected = len(near) * (1 + jnp.where(has_following, 1, 0) + jnp.where(has_previous, 1, 0))
    pl.semaphore_wait(barrier, expected)

    class Gather:
        def __init__(self, ref, rows, split, lead=None):
            self.parts = [(ref, slice(0, rows), split)]
            if lead is not None:
                self.parts = [(lead, slice(0, 1), None)] + self.parts
            self.near = {}
            self.far = {}
            self.sib = {}

        def begin(self):
            for offset in (2, -2, 1, -1):
                slot = (-offset) % CHIPS
                for n, (ref, rows, _) in enumerate(self.parts):
                    self.near[slot, n] = send(ref.at[0, rows, mine], ref.at[slot, rows, mine], chip(offset))
                if offset == 2:
                    self.share(0)

        def begin_next(self, src, first):
            for offset in (2, -2, 0, 1, -1):
                slot = (-offset) % CHIPS
                ref = self.parts[0][0]
                arrival = counter[0]
                copy = send(src, ref.at[slot, :, mine], following(offset), has_following)
                if offset == 0:
                    self.own = copy
                else:
                    self.near[slot, 0] = copy
                    send(first, ref.at[slot, :, mine], chip(offset), no_previous, arrival)

        def share_own(self, first):
            ref = self.parts[0][0]

            @pl.when(has_previous)
            def _():
                self.own.wait_recv()

            @pl.when(no_previous)
            def _():
                ref[0, :, mine] = first[...]

            self.share(0)

        def share(self, slot):
            for n, (ref, rows, _) in enumerate(self.parts):
                self.sib[slot, n] = send(ref.at[slot, rows, mine], ref.at[slot, rows, mine], sibling)

        def pass_on(self):
            for held, step, low in ((6, 1, True), (2, -1, False)):
                for n, (ref, rows, split) in enumerate(self.parts):
                    self.near[held, n].wait_recv()
                    slot = (held - step) % CHIPS
                    self.far[slot, n] = [send(ref.at[held, rows, mine], ref.at[slot, rows, mine], chip(step))]
                    if split is None:
                        if low:
                            self.far[4, n] = [send(ref.at[held, rows, mine], ref.at[4, rows, mine], chip(2))]
                    else:
                        part = slice(0, split) if low else slice(split, rows.stop)
                        self.far.setdefault((4, n), []).append(
                            send(ref.at[held, part, mine], ref.at[4, part, mine], chip(2 * step))
                        )
                self.share(held)

        def share_near(self):
            for slot in (7, 1):
                for n in range(len(self.parts)):
                    self.near[slot, n].wait_recv()
                self.share(slot)

        def share_far(self):
            for slot in (5, 3, 4):
                for n in range(len(self.parts)):
                    for copy in self.far[slot, n]:
                        copy.wait_recv()
                self.share(slot)

        def ready(self, slot):
            for n in range(len(self.parts)):
                self.sib[slot, n].wait_recv()

    def base_of(slot):
        return pl.multiple_of(lax.rem(y + slot, CHIPS) * PAIR, PAIR)

    def build(slot, norms):
        base = base_of(slot)
        for part in range(3):
            lanes = slice(part * 256, (part + 1) * 256)
            rows = pl.ds(pl.multiple_of(base + part * 256, 256), 256)
            direction = fz[rows, :].astype(F32) + dot_tn(g0[slot, TOK : TOK + RANK, lanes], aout[...])
            w[rows, :] = direction.astype(BF16)
            norms = norms + jnp.sum((direction * direction).reshape(32, 8, COLS), axis=0)
        return norms

    def chunk(ref, slot, squares, total, with_adapter=False):
        z = ref[slot, 0:TOK, :].astype(F32)
        squares = squares + lane_groups(z * z)
        scaled = (z * gn[slot, 0:1, :]).astype(BF16)
        if with_adapter:
            scaled = jnp.concatenate([scaled, ref[slot, TOK : TOK + RANK, :]], axis=0)
        total = total + dot(scaled, w[pl.ds(base_of(slot), PAIR), :])
        return squares, total

    def rscale_of(squares):
        return lax.rsqrt(jnp.sum(squares, axis=1, keepdims=True) / FEATURES + 1e-05)

    def normalise(ref, out, rscale):
        for slot in range(CHIPS):
            z = ref[slot, 0:TOK, :].astype(F32)
            out[slot] = (z * rscale * gn[slot, 0:1, :]).astype(BF16)

    def slope_of(preact):
        sig = 1.0 / (1.0 + jnp.exp(-preact))
        return sig * (1.0 + preact * (1.0 - sig))

    class Scatter:
        def __init__(self, rows, split, pb, sb, sv, rv, back):
            self.rows, self.split = rows, split
            self.pb, self.sb, self.sv, self.rv, self.back = pb, sb, sv, rv, back

        def prepare(self, lhs, ref, rscale, dots, extra=None):
            self.args = lhs, ref, rscale, rscale * rscale * dots / FEATURES, extra

        def compute(self, start, stop):
            lhs, ref, rscale, tilt, extra = self.args
            for n in range(start, stop):
                slot = ORDER[n]
                value = dot_nt(lhs, w[pl.ds(base_of(slot), PAIR), :])
                z = ref[slot, 0:TOK, :].astype(F32)
                scaled = value[0:TOK] * rscale
                term = jnp.sum(scaled * z, axis=0, keepdims=True)
                gt[n : n + 1, :] = term if extra is None else gt[n : n + 1, :] + term
                result = scaled * gn[slot, 0:1, :] - z * tilt
                if extra is not None:
                    result = jnp.concatenate([result, value[TOK:] + extra(slot)], axis=0)
                self.pb[n] = result.astype(BF16)
            return send(self.pb.at[start:stop, :, other], self.sb.at[start:stop], sibling)

        def compute_first(self):
            self.first = self.compute(0, 3)

        def compute_second(self):
            self.second = self.compute(3, 8)

        def pair_sum(self, n):
            return self.pb[n, :, mine].astype(F32) + self.sb[n].astype(F32)

        def deliver(self, n, offset):
            src, dst = self.sv.at[n], self.rv.at[n]
            if self.back:
                return send(src, dst, previous(offset), has_previous)
            return send(src, dst, chip(offset))

        def stage_one(self):
            rv, sv = self.rv, self.sv
            self.first.wait_recv()
            sv[2] = self.pair_sum(2).astype(BF16)
            low, high = slice(0, self.split), slice(self.split, self.rows)
            self.r4a = send(sv.at[2, low], rv.at[2, low], chip(-2))
            self.r4b = send(sv.at[2, high], rv.at[2, high], chip(2))
            sv[0] = self.pair_sum(0).astype(BF16)
            self.r1 = send(sv.at[0], rv.at[0], chip(1))
            sv[1] = self.pair_sum(1).astype(BF16)
            self.r2 = send(sv.at[1], rv.at[1], chip(-1))

        def stage_one_direct(self):
            self.second.wait_recv()
            self.last = []
            for n, offset in ((3, 1), (4, -1)):
                self.sv[n] = self.pair_sum(n).astype(BF16)
                self.last.append(self.deliver(n, offset))
            if self.back:
                self.sv[7] = self.pair_sum(7).astype(BF16)
                self.last.append(self.deliver(7, 0))

        def stage_two(self):
            rv, split = self.rv, self.split
            self.r1.wait_recv()
            self.r4b.wait_recv()
            total = self.pair_sum(5) + rv[0].astype(F32)
            total = jnp.concatenate([total[0:split], total[split:] + rv[2, split:].astype(F32)], axis=0)
            self.sv[5] = total.astype(BF16)
            self.last.append(self.deliver(5, 2))
            self.r2.wait_recv()
            self.r4a.wait_recv()
            total = self.pair_sum(6) + rv[1].astype(F32)
            total = jnp.concatenate([total[0:split] + rv[2, 0:split].astype(F32), total[split:]], axis=0)
            self.sv[6] = total.astype(BF16)
            self.last.append(self.deliver(6, -2))

        def final(self):
            for copy in self.last:
                copy.wait_recv()
            total = self.rv[7].astype(F32) if self.back else self.pair_sum(7)
            for n in (3, 4, 5, 6):
                total = total + self.rv[n].astype(F32)
            return total

    class RowScatter:
        def compute(self):
            self.sib = send(gt.at[:, other], gts, sibling)

        def row(self, n, offset):
            return send(gtv.at[n : n + 1], gtr.at[n : n + 1], chip(offset))

        def stage_one(self):
            self.sib.wait_recv()
            gtv[...] = gt[:, mine] + gts[...]
            self.inner = [self.row(0, 1), self.row(1, -1), self.row(2, -2)]
            self.last = [self.row(3, 1), self.row(4, -1)]

        def stage_two(self):
            for copy in self.inner:
                copy.wait_recv()
            gtv[5:6] = gtv[5:6] + gtr[0:1]
            gtv[6:7] = gtv[6:7] + gtr[1:2] + gtr[2:3]
            self.last += [self.row(5, 2), self.row(6, -2)]

        def final(self):
            for copy in self.last:
                copy.wait_recv()
            return gtv[7:8] + gtr[3:4] + gtr[4:5] + gtr[5:6] + gtr[6:7]

    ga_s0 = Gather(g0, TOK + RANK, 48, lead=gn)
    ga_t0 = Gather(g1, TOK, 32)
    ga_s1 = Gather(g2, TOK, 32)
    ga_t1 = Gather(g3, TOK, 32)
    rs0 = Scatter(TOK, 32, pb0, sb0, sv0, rv0, True)
    rs1 = Scatter(TOK + RANK, 48, pb1, sb1, sv1, rv1, False)
    rows = RowScatter()

    def fresh():
        return jnp.zeros((TOK, 128), F32), jnp.zeros((TOK, COLS), F32)

    l_s0.wait()
    l_a.wait()
    ga_s0.begin()
    l_tg.wait()
    early_cot = send(tg, tgx, previous(0), has_previous)
    l_fz.wait()
    l_p.wait()
    norms = jnp.zeros((8, COLS), F32)
    squares = jnp.zeros((TOK, 128), F32)
    total = jnp.zeros((TOK + RANK, COLS), F32)
    ga_s0.ready(0)
    norms = build(0, norms)
    squares, total = chunk(g0, 0, squares, total, True)
    ga_s0.pass_on()
    l_t0.wait()
    ga_t0.begin()
    ga_s0.share_near()
    for slot in (6, 2, 7, 1):
        ga_s0.ready(slot)
        norms = build(slot, norms)
        squares, total = chunk(g0, slot, squares, total, True)
    ga_s0.share_far()
    ga_t0.pass_on()
    l_s1.wait()
    ga_s1.begin()
    for slot in (5, 3, 4):
        ga_s0.ready(slot)
        norms = build(slot, norms)
        squares, total = chunk(g0, slot, squares, total, True)
    norm_squares = jnp.sum(norms, axis=0, keepdims=True) + 1e-06
    colnorm = jnp.sqrt(norm_squares)
    col_scale = mag_ref[...] / colnorm
    r0 = rscale_of(squares)
    raw0 = total[0:TOK] * r0
    adapter_direction = total[TOK:]
    preact = raw0 * col_scale
    pg = tg[...].astype(F32) * slope_of(preact)
    pgs0 = (pg * col_scale).astype(BF16)
    inner = jnp.sum(pg * raw0, axis=0, keepdims=True)
    rs0.prepare(pgs0, g0, r0, jnp.sum(pg * preact, axis=1, keepdims=True))
    rs0.compute_first()
    rs0.compute_second()
    ga_t0.share_near()
    ga_s1.pass_on()
    rs0.stage_one()
    ga_t0.share_far()
    squares, total = fresh()
    for slot in (0, 6, 2, 7, 1):
        ga_t0.ready(slot)
        squares, total = chunk(g1, slot, squares, total)
    rs0.stage_one_direct()
    for slot in (5, 3, 4):
        ga_t0.ready(slot)
        squares, total = chunk(g1, slot, squares, total)
    preact = total * rscale_of(squares) * col_scale
    em[...] = (g1[0, :, mine].astype(F32) + preact / (1.0 + jnp.exp(-preact))).astype(BF16)
    l_ent.wait()
    ga_t1.begin_next(em, ent)
    ga_s1.share_near()
    rs0.stage_two()
    normalise(g0, zn0, r0)
    factor = aout[...]
    weights0 = dot_nt(factor, pgs0)
    ga_s1.share_far()
    squares1, total1 = fresh()
    for slot in (0, 6, 2, 7, 1):
        ga_s1.ready(slot)
        squares1, total1 = chunk(g2, slot, squares1, total1)
    for slot in (5, 3, 4):
        ga_s1.ready(slot)
        squares1, total1 = chunk(g2, slot, squares1, total1)
    r1 = rscale_of(squares1)
    raw1 = total1 * r1
    preact1 = raw1 * col_scale
    slope = slope_of(preact1)
    normalise(g2, zn1, r1)
    ga_t1.share_own(ent)
    ga_t1.pass_on()
    l_ret.wait()

    @pl.when(has_following)
    def _():
        early_cot.wait_recv()
        gx[...] = (tgx[...].astype(F32) + rs0.final()).astype(BF16)

    @pl.when(jnp.logical_not(has_following))
    def _():
        gx[...] = ret[...]

    cot1 = gx[...].astype(F32)
    pg = cot1 * slope
    pgs1 = (pg * col_scale).astype(BF16)
    inner = inner + jnp.sum(pg * raw1, axis=0, keepdims=True)
    scaled_ratio = col_scale * inner / norm_squares
    weights = jnp.concatenate([weights0, dot_nt(factor, pgs1)], axis=1).astype(BF16)
    shrunk = (factor.astype(F32) * -scaled_ratio).astype(BF16)

    def column_extra(slot):
        return dot(weights, jnp.concatenate([zn0[slot], zn1[slot]], axis=0))

    rs1.prepare(
        jnp.concatenate([pgs1, shrunk], axis=0), g2, r1, jnp.sum(pg * preact1, axis=1, keepdims=True), column_extra
    )
    rs1.compute_first()
    rs1.compute_second()
    rows.compute()
    rs1.stage_one()
    rs1.stage_one_direct()
    rows.stage_one()
    ga_t1.share_near()
    mag_o[...] = inner / colnorm
    product = jnp.zeros((RANK, TOK * SLOTS), F32)
    for slot in range(CHIPS):
        product = product + dot_nt(
            g0[slot, TOK : TOK + RANK, :], jnp.concatenate([zn0[slot], zn1[slot]], axis=0)
        )
    upper = product.astype(BF16)
    lower = (product - upper.astype(F32)).astype(BF16)
    both = dot(jnp.concatenate([upper, lower], axis=0), jnp.concatenate([pgs0, pgs1], axis=0))
    gout_o[0] = both[0:RANK] + both[RANK:] - adapter_direction * scaled_ratio
    squares, total = fresh()
    for slot in (0, 6, 2, 7, 1):
        ga_t1.ready(slot)
        squares, total = chunk(g3, slot, squares, total)
    ga_t1.share_far()
    rs1.stage_two()
    rows.stage_two()
    for slot in (5, 3, 4):
        ga_t1.ready(slot)
        squares, total = chunk(g3, slot, squares, total)
    preact = total * rscale_of(squares) * col_scale
    act_o[0] = g3[0, :, mine].astype(F32) + preact / (1.0 + jnp.exp(-preact))
    gain_o[...] = rows.final()
    result = rs1.final()
    gin_o[0] = result[TOK:]
    grad_o[0] = cot1 + result[0:TOK]
    for copy, condition in started:
        if condition is None:
            copy.wait_send()
        else:
            pl.when(condition)(copy.wait_send)


def local(*args):
    hbm = pl.BlockSpec(memory_space=pltpu.HBM)
    vmem = pl.BlockSpec(memory_space=pltpu.VMEM)
    rows1 = TOK + RANK

    def scatter_buffers(rows):
        return [
            pltpu.VMEM((8, rows, PAIR), BF16),
            pltpu.VMEM((8, rows, COLS), BF16),
            pltpu.VMEM((8, rows, COLS), BF16),
            pltpu.VMEM((8, rows, COLS), BF16),
        ]

    gathered = pltpu.VMEM((CHIPS, TOK, PAIR), BF16)
    block = pltpu.VMEM((TOK, COLS), BF16)
    out_shape = (
        jax.ShapeDtypeStruct((1, TOK, COLS), F32),
        jax.ShapeDtypeStruct((1, TOK, COLS), F32),
        jax.ShapeDtypeStruct((1, COLS), F32),
        jax.ShapeDtypeStruct((1, RANK, COLS), F32),
        jax.ShapeDtypeStruct((1, RANK, COLS), F32),
        jax.ShapeDtypeStruct((1, COLS), F32),
    )
    act, grad, *sums = pl.pallas_call(
        kernel,
        out_shape=out_shape,
        in_specs=[hbm] * 8 + [vmem] * 2,
        out_specs=(vmem,) * 6,
        scratch_shapes=[
            pltpu.VMEM((FEATURES, COLS), BF16),
            pltpu.VMEM((FEATURES, COLS), BF16),
            pltpu.VMEM((CHIPS, rows1, PAIR), BF16),
            gathered,
            gathered,
            gathered,
            pltpu.VMEM((CHIPS, 8, PAIR), F32),
            gathered,
            gathered,
            block,
            block,
            block,
            block,
            pltpu.VMEM((RANK, COLS), BF16),
            block,
            block,
            *scatter_buffers(TOK),
            *scatter_buffers(rows1),
            pltpu.VMEM((8, PAIR), F32),
            pltpu.VMEM((8, COLS), F32),
            pltpu.VMEM((8, COLS), F32),
            pltpu.VMEM((8, COLS), F32),
            pltpu.SemaphoreType.DMA((COPIES,)),
            pltpu.SemaphoreType.DMA((COPIES,)),
            pltpu.SemaphoreType.DMA((9,)),
        ],
        compiler_params=pltpu.CompilerParams(
            collective_id=0, has_side_effects=True, vmem_limit_bytes=56 * 2**20
        ),
        name="window",
    )(*args)
    mean = 1.0 / (SLOTS * TOK)
    return act.astype(BF16), grad.astype(BF16), *[total * mean for total in sums]


def solution(mesh):
    in_specs = (
        P("section", None, "tensor"),
        P(None, None, "tensor"),
        P("section", None, None, "tensor"),
        P("section", None, "tensor"),
        P(None, None, "tensor"),
        P("section", None, "tensor"),
        P("section", None, "tensor"),
        P("section", None, "tensor"),
        P("section", "tensor"),
        P("section", "tensor"),
    )
    out_specs = (
        P("section", None, "tensor"),
        P("section", None, "tensor"),
        P("section", "tensor"),
        P("section", None, "tensor"),
        P("section", None, "tensor"),
        P("section", "tensor"),
    )
    return jax.shard_map(local, mesh=mesh, in_specs=in_specs, out_specs=out_specs, check_vma=False)
```

time: 80.1 us -> 63 us (0.79)
  the two profiles are of different devices: /device:TPU:1 before, /device:TPU:198 now
where the time goes in v2:
time: 63 us; the launch traced here: 62.7 us
  Pallas kernels  56.4 us (90%)
  other arithmetic  5.66 us (9%)
  between operations  0.65 us (1%)
    pallas_call x1, Pallas kernels, local(): pl.pallas_call(kernel, out_shape=out_shape, in_specs=[hbm] * 8 + [vmem] *...  56.4 us
    mul x2, other arithmetic, local(): total * mean  2.62 us
    convert_element_type x1, other arithmetic, local(): act.astype(BF16)  1.52 us
    convert_element_type x1, other arithmetic, local(): grad.astype(BF16)  1.52 us

profile of v2, /device:TPU:198, one launch (start us, length us, event | category | flops | bytes accessed | tf_op | source)
XLA Modules:
  0.0 62.7 jit_solution(11048916231168931921)
XLA Ops:
  0.6 56.4 %window.1 = (f32[1,64,384]{2,1,0:T(8,128)}, f32[1,64,384]{2,1,0:T(8,128)}, f32[1,384]{1,0:T(1,128)}, f32[1,16,384]{2,1,0:T(8,128)}, f32[1,16,384]{2,1,0:T(8,128)}, /*index=5*/f32[1,384]{1,0:T(1,128)}) custom-call(bf16[1,64,384]{2,1,0:T(8,128)(2,1)} %act_hbm.1, bf16[1,64,384]{2,1,0:T(8,128)(2,1)} %ent_hbm.1, bf16[1,2,64,384]{3,2,1,0:T(8,128)(2,1)} %sta_hbm.1, ...), custom_call_target="tpu_custom_call" | custom-call | tf_op jit(solution)/shard_map/window/pallas_call | solution.py:525
  57.0 1.5 %convert_element_type.6 = bf16[1,64,384]{2,1,0:T(8,128)(2,1)} convert(f32[1,64,384]{2,1,0:T(8,128)} %get-tuple-element.12) | non-fusion elementwise | flops 24576 | bytes 147456 | tf_op jit(solution)/shard_map/convert_element_type | solution.py:563
  58.5 1.2 %broadcast_multiply_fusion.2 = (f32[1,384]{1,0:T(1,128)}, f32[1,384]{1,0:T(1,128)}) fusion(f32[1,384]{1,0:T(1,128)} %get-tuple-element.17, f32[1,384]{1,0:T(1,128)} %get-tuple-element.14), kind=kLoop, calls=%fused_computation.2 | loop fusion | flops 768 | bytes 6144 | tf_op jit(solution)/shard_map/mul | solution.py:563
  59.8 1.5 %convert_element_type.7 = bf16[1,64,384]{2,1,0:T(8,128)(2,1)} convert(f32[1,64,384]{2,1,0:T(8,128)} %get-tuple-element.13) | non-fusion elementwise | flops 24576 | bytes 147456 | tf_op jit(solution)/shard_map/convert_element_type | solution.py:563
  61.3 1.4 %broadcast_multiply_fusion = (f32[1,16,384]{2,1,0:T(8,128)}, f32[1,16,384]{2,1,0:T(8,128)}) fusion(f32[1,16,384]{2,1,0:T(8,128)} %get-tuple-element.16, f32[1,16,384]{2,1,0:T(8,128)} %get-tuple-element.15), kind=kLoop, calls=%fused_computation | loop fusion | flops 12288 | bytes 98304 | tf_op jit(solution)/shard_map/mul | solution.py:563

commit v3 on v2

--- a/solution.py
+++ b/solution.py
@@ -1,3 +1,5 @@
+import math
+
 import jax
 import jax.numpy as jnp
 from jax import lax
@@ -16,7 +18,8 @@
 FEATURES = CHIPS * PAIR
 SLOTS = 2
 ORDER = (3, 5, 4, 1, 7, 2, 6, 0)
-COPIES = 160
+ARRIVALS = 90
+DEPARTURES = 30
 
 
 def dot(a, b):
@@ -40,7 +43,7 @@
 
 def kernel(
     act_hbm, ent_hbm, sta_hbm, tg_hbm, ret_hbm, frozen_hbm, ain_hbm, aout_hbm, mag_ref, gain_ref,
-    act_o, grad_o, mag_o, gin_o, gout_o, gain_o,
+    packed,
     fz, w, g0, g1, g2, g3, gn, zn0, zn1, tg, tgx, ent, ret, aout, em, gx,
     pb0, sb0, sv0, rv0, pb1, sb1, sv1, rv1, gt, gts, gtv, gtr, ssem, rsem, lsem,
 ):
@@ -65,24 +68,42 @@
     has_previous = sec > 0
     has_following = sec < sections - 1
     no_previous = jnp.logical_not(has_previous)
-
-    counter = [0]
-    started = []
-
-    def send(src, dst, device, condition=None, arrival=None):
-        index = counter[0]
-        counter[0] += 1
-        arrival = index if arrival is None else arrival
+    conditions = (None, has_previous, has_following, no_previous)
+
+    arrivals = [0]
+    departures = [4]
+    sent = [0, 0, 0, 0]
+    alone = []
+
+    class Arrival:
+        def __init__(self, ref):
+            self.ref, self.index, self.waited = ref, arrivals[0], False
+            arrivals[0] += 1
+
+        def wait(self):
+            if not self.waited:
+                pltpu.make_async_copy(self.ref, self.ref, rsem.at[self.index]).wait()
+            self.waited = True
+
+    def send(src, dst, device, arrival=None, kind=0):
+        arrival = Arrival(dst) if arrival is None else arrival
+        if kind is None:
+            index = departures[0]
+            departures[0] += 1
+        else:
+            index = kind
+            sent[kind] += math.prod(src.shape) // COLS
         copy = pltpu.make_async_remote_copy(
-            src_ref=src, dst_ref=dst, send_sem=ssem.at[index], recv_sem=rsem.at[arrival],
+            src_ref=src, dst_ref=dst, send_sem=ssem.at[index], recv_sem=rsem.at[arrival.index],
             device_id=device, device_id_type=MESH,
         )
-        if condition is None:
+        if kind is None:
+            alone.append(copy)
+        if kind:
+            pl.when(conditions[kind])(copy.start)
+        else:
             copy.start()
-        else:
-            pl.when(condition)(copy.start)
-        started.append((copy, condition))
-        return copy
+        return arrival
 
     locals_ = []
 
@@ -125,83 +146,91 @@
     pl.semaphore_wait(barrier, expected)
 
     class Gather:
+        groups = {0: (0,), 6: (6, 2), 2: (6, 2), 7: (7, 1), 1: (7, 1), 5: (5, 3, 4), 3: (5, 3, 4), 4: (5, 3, 4)}
+
         def __init__(self, ref, rows, split, lead=None):
-            self.parts = [(ref, slice(0, rows), split)]
-            if lead is not None:
-                self.parts = [(lead, slice(0, 1), None)] + self.parts
-            self.near = {}
-            self.far = {}
-            self.sib = {}
+            self.ref, self.rows, self.split, self.lead = ref, slice(0, rows), split, lead
+            self.near, self.far, self.lead_in = {}, {}, {}
+            self.far4 = Arrival(ref.at[4, self.rows, mine])
+            self.shared, self.lead_shared = {}, {}
+            for group in ((0,), (6, 2), (7, 1), (5, 3, 4)):
+                span = slice(3, 6) if len(group) == 3 else slice(0, len(group))
+                arrival = Arrival(ref.at[span, self.rows, mine])
+                self.shared.update({slot: arrival for slot in group})
+
+        def block(self, slot, rows=None):
+            return self.ref.at[slot, self.rows if rows is None else rows, mine]
+
+        def lead_row(self, slot):
+            return self.lead.at[slot, 0:1, mine]
 
         def begin(self):
             for offset in (2, -2, 1, -1):
                 slot = (-offset) % CHIPS
-                for n, (ref, rows, _) in enumerate(self.parts):
-                    self.near[slot, n] = send(ref.at[0, rows, mine], ref.at[slot, rows, mine], chip(offset))
+                if self.lead is not None:
+                    self.lead_in[slot] = send(self.lead_row(0), self.lead_row(slot), chip(offset), kind=None)
+                self.near[slot] = send(self.block(0), self.block(slot), chip(offset))
                 if offset == 2:
                     self.share(0)
 
         def begin_next(self, src, first):
             for offset in (2, -2, 0, 1, -1):
                 slot = (-offset) % CHIPS
-                ref = self.parts[0][0]
-                arrival = counter[0]
-                copy = send(src, ref.at[slot, :, mine], following(offset), has_following)
+                arrival = send(src, self.block(slot), following(offset), kind=2)
                 if offset == 0:
-                    self.own = copy
+                    self.own = arrival
                 else:
-                    self.near[slot, 0] = copy
-                    send(first, ref.at[slot, :, mine], chip(offset), no_previous, arrival)
+                    self.near[slot] = arrival
+                    send(first, self.block(slot), chip(offset), arrival, kind=3)
 
         def share_own(self, first):
-            ref = self.parts[0][0]
-
             @pl.when(has_previous)
             def _():
-                self.own.wait_recv()
+                self.own.wait()
 
             @pl.when(no_previous)
             def _():
-                ref[0, :, mine] = first[...]
+                self.ref[0, self.rows, mine] = first[...]
 
             self.share(0)
 
         def share(self, slot):
-            for n, (ref, rows, _) in enumerate(self.parts):
-                self.sib[slot, n] = send(ref.at[slot, rows, mine], ref.at[slot, rows, mine], sibling)
+            if self.lead is not None:
+                self.lead_shared[slot] = send(self.lead_row(slot), self.lead_row(slot), sibling, kind=None)
+            send(self.block(slot), self.block(slot), sibling, self.shared[slot])
 
         def pass_on(self):
-            for held, step, low in ((6, 1, True), (2, -1, False)):
-                for n, (ref, rows, split) in enumerate(self.parts):
-                    self.near[held, n].wait_recv()
-                    slot = (held - step) % CHIPS
-                    self.far[slot, n] = [send(ref.at[held, rows, mine], ref.at[slot, rows, mine], chip(step))]
-                    if split is None:
-                        if low:
-                            self.far[4, n] = [send(ref.at[held, rows, mine], ref.at[4, rows, mine], chip(2))]
-                    else:
-                        part = slice(0, split) if low else slice(split, rows.stop)
-                        self.far.setdefault((4, n), []).append(
-                            send(ref.at[held, part, mine], ref.at[4, part, mine], chip(2 * step))
-                        )
+            for held, step in ((6, 1), (2, -1)):
+                slot = (held - step) % CHIPS
+                if self.lead is not None:
+                    self.lead_in[held].wait()
+                    self.lead_in[slot] = send(self.lead_row(held), self.lead_row(slot), chip(step), kind=None)
+                    if step == 1:
+                        self.lead_in[4] = send(self.lead_row(held), self.lead_row(4), chip(2), kind=None)
+                self.near[held].wait()
+                self.far[slot] = send(self.block(held), self.block(slot), chip(step))
+                part = slice(0, self.split) if step == 1 else slice(self.split, self.rows.stop)
+                send(self.block(held, part), self.block(4, part), chip(2 * step), self.far4)
                 self.share(held)
 
         def share_near(self):
             for slot in (7, 1):
-                for n in range(len(self.parts)):
-                    self.near[slot, n].wait_recv()
+                self.near[slot].wait()
+                if self.lead is not None:
+                    self.lead_in[slot].wait()
                 self.share(slot)
 
         def share_far(self):
             for slot in (5, 3, 4):
-                for n in range(len(self.parts)):
-                    for copy in self.far[slot, n]:
-                        copy.wait_recv()
+                (self.far4 if slot == 4 else self.far[slot]).wait()
+                if self.lead is not None:
+                    self.lead_in[slot].wait()
                 self.share(slot)
 
         def ready(self, slot):
-            for n in range(len(self.parts)):
-                self.sib[slot, n].wait_recv()
+            self.shared[slot].wait()
+            if self.lead is not None:
+                self.lead_shared[slot].wait()
 
     def base_of(slot):
         return pl.multiple_of(lax.rem(y + slot, CHIPS) * PAIR, PAIR)
@@ -272,12 +301,13 @@
         def deliver(self, n, offset):
             src, dst = self.sv.at[n], self.rv.at[n]
             if self.back:
-                return send(src, dst, previous(offset), has_previous)
-            return send(src, dst, chip(offset))
+                send(src, dst, previous(offset), self.last, kind=1)
+            else:
+                send(src, dst, chip(offset), self.last)
 
         def stage_one(self):
             rv, sv = self.rv, self.sv
-            self.first.wait_recv()
+            self.first.wait()
             sv[2] = self.pair_sum(2).astype(BF16)
             low, high = slice(0, self.split), slice(self.split, self.rows)
             self.r4a = send(sv.at[2, low], rv.at[2, low], chip(-2))
@@ -288,33 +318,32 @@
             self.r2 = send(sv.at[1], rv.at[1], chip(-1))
 
         def stage_one_direct(self):
-            self.second.wait_recv()
-            self.last = []
+            self.second.wait()
+            self.last = Arrival(self.rv.at[3:8] if self.back else self.rv.at[3:7])
             for n, offset in ((3, 1), (4, -1)):
                 self.sv[n] = self.pair_sum(n).astype(BF16)
-                self.last.append(self.deliver(n, offset))
+                self.deliver(n, offset)
             if self.back:
                 self.sv[7] = self.pair_sum(7).astype(BF16)
-                self.last.append(self.deliver(7, 0))
+                self.deliver(7, 0)
 
         def stage_two(self):
             rv, split = self.rv, self.split
-            self.r1.wait_recv()
-            self.r4b.wait_recv()
+            self.r1.wait()
+            self.r4b.wait()
             total = self.pair_sum(5) + rv[0].astype(F32)
             total = jnp.concatenate([total[0:split], total[split:] + rv[2, split:].astype(F32)], axis=0)
             self.sv[5] = total.astype(BF16)
-            self.last.append(self.deliver(5, 2))
-            self.r2.wait_recv()
-            self.r4a.wait_recv()
+            self.deliver(5, 2)
+            self.r2.wait()
+            self.r4a.wait()
             total = self.pair_sum(6) + rv[1].astype(F32)
             total = jnp.concatenate([total[0:split] + rv[2, 0:split].astype(F32), total[split:]], axis=0)
             self.sv[6] = total.astype(BF16)
-            self.last.append(self.deliver(6, -2))
+            self.deliver(6, -2)
 
         def final(self):
-            for copy in self.last:
-                copy.wait_recv()
+            self.last.wait()
             total = self.rv[7].astype(F32) if self.back else self.pair_sum(7)
             for n in (3, 4, 5, 6):
                 total = total + self.rv[n].astype(F32)
@@ -322,27 +351,27 @@
 
     class RowScatter:
         def compute(self):
-            self.sib = send(gt.at[:, other], gts, sibling)
+            self.sib = send(gt.at[:, other], gts, sibling, kind=None)
 
         def row(self, n, offset):
-            return send(gtv.at[n : n + 1], gtr.at[n : n + 1], chip(offset))
+            return send(gtv.at[n : n + 1], gtr.at[n : n + 1], chip(offset), kind=None)
 
         def stage_one(self):
-            self.sib.wait_recv()
+            self.sib.wait()
             gtv[...] = gt[:, mine] + gts[...]
             self.inner = [self.row(0, 1), self.row(1, -1), self.row(2, -2)]
             self.last = [self.row(3, 1), self.row(4, -1)]
 
         def stage_two(self):
             for copy in self.inner:
-                copy.wait_recv()
+                copy.wait()
             gtv[5:6] = gtv[5:6] + gtr[0:1]
             gtv[6:7] = gtv[6:7] + gtr[1:2] + gtr[2:3]
             self.last += [self.row(5, 2), self.row(6, -2)]
 
         def final(self):
             for copy in self.last:
-                copy.wait_recv()
+                copy.wait()
             return gtv[7:8] + gtr[3:4] + gtr[4:5] + gtr[5:6] + gtr[6:7]
 
     ga_s0 = Gather(g0, TOK + RANK, 48, lead=gn)
@@ -360,7 +389,7 @@
     l_a.wait()
     ga_s0.begin()
     l_tg.wait()
-    early_cot = send(tg, tgx, previous(0), has_previous)
+    early_cot = send(tg, tgx, previous(0), kind=1)
     l_fz.wait()
     l_p.wait()
     norms = jnp.zeros((8, COLS), F32)
@@ -438,7 +467,7 @@
 
     @pl.when(has_following)
     def _():
-        early_cot.wait_recv()
+        early_cot.wait()
         gx[...] = (tgx[...].astype(F32) + rs0.final()).astype(BF16)
 
     @pl.when(jnp.logical_not(has_following))
@@ -466,7 +495,8 @@
     rs1.stage_one_direct()
     rows.stage_one()
     ga_t1.share_near()
-    mag_o[...] = inner / colnorm
+    packed[160:168] = jnp.zeros((8, COLS), F32)
+    packed[160:161] = inner / colnorm
     product = jnp.zeros((RANK, TOK * SLOTS), F32)
     for slot in range(CHIPS):
         product = product + dot_nt(
@@ -475,7 +505,7 @@
     upper = product.astype(BF16)
     lower = (product - upper.astype(F32)).astype(BF16)
     both = dot(jnp.concatenate([upper, lower], axis=0), jnp.concatenate([pgs0, pgs1], axis=0))
-    gout_o[0] = both[0:RANK] + both[RANK:] - adapter_direction * scaled_ratio
+    packed[144:160] = both[0:RANK] + both[RANK:] - adapter_direction * scaled_ratio
     squares, total = fresh()
     for slot in (0, 6, 2, 7, 1):
         ga_t1.ready(slot)
@@ -487,16 +517,30 @@
         ga_t1.ready(slot)
         squares, total = chunk(g3, slot, squares, total)
     preact = total * rscale_of(squares) * col_scale
-    act_o[0] = g3[0, :, mine].astype(F32) + preact / (1.0 + jnp.exp(-preact))
-    gain_o[...] = rows.final()
+    packed[0:64] = g3[0, :, mine].astype(F32) + preact / (1.0 + jnp.exp(-preact))
+    packed[161:162] = rows.final()
     result = rs1.final()
-    gin_o[0] = result[TOK:]
-    grad_o[0] = cot1 + result[0:TOK]
-    for copy, condition in started:
+    packed[128:144] = result[TOK:]
+    packed[64:128] = cot1 + result[0:TOK]
+    for copy in alone:
+        copy.wait_send()
+    for kind, condition in enumerate(conditions):
+        everything = w.at[0 : sent[kind]]
+        copy = pltpu.make_async_copy(everything, everything, ssem.at[kind])
         if condition is None:
-            copy.wait_send()
+            copy.wait()
         else:
-            pl.when(condition)(copy.wait_send)
+            pl.when(condition)(copy.wait)
+
+
+def hand_out(packed, act, grad, mag, grad_in, grad_out, gain):
+    mean = 1.0 / (SLOTS * TOK)
+    act[0] = packed[0:64].astype(BF16)
+    grad[0] = packed[64:128].astype(BF16)
+    grad_in[0] = packed[128:144] * mean
+    grad_out[0] = packed[144:160] * mean
+    mag[...] = packed[160:161] * mean
+    gain[...] = packed[161:162] * mean
 
 
 def local(*args):
@@ -515,18 +559,18 @@
     gathered = pltpu.VMEM((CHIPS, TOK, PAIR), BF16)
     block = pltpu.VMEM((TOK, COLS), BF16)
     out_shape = (
-        jax.ShapeDtypeStruct((1, TOK, COLS), F32),
-        jax.ShapeDtypeStruct((1, TOK, COLS), F32),
+        jax.ShapeDtypeStruct((1, TOK, COLS), BF16),
+        jax.ShapeDtypeStruct((1, TOK, COLS), BF16),
         jax.ShapeDtypeStruct((1, COLS), F32),
         jax.ShapeDtypeStruct((1, RANK, COLS), F32),
         jax.ShapeDtypeStruct((1, RANK, COLS), F32),
         jax.ShapeDtypeStruct((1, COLS), F32),
     )
-    act, grad, *sums = pl.pallas_call(
+    packed = pl.pallas_call(
         kernel,
-        out_shape=out_shape,
+        out_shape=jax.ShapeDtypeStruct((168, COLS), F32),
         in_specs=[hbm] * 8 + [vmem] * 2,
-        out_specs=(vmem,) * 6,
+        out_specs=vmem,
         scratch_shapes=[
             pltpu.VMEM((FEATURES, COLS), BF16),
             pltpu.VMEM((FEATURES, COLS), BF16),
@@ -550,8 +594,8 @@
             pltpu.VMEM((8, COLS), F32),
             pltpu.VMEM((8, COLS), F32),
             pltpu.VMEM((8, COLS), F32),
-            pltpu.SemaphoreType.DMA((COPIES,)),
-            pltpu.SemaphoreType.DMA((COPIES,)),
+            pltpu.SemaphoreType.DMA((DEPARTURES,)),
+            pltpu.SemaphoreType.DMA((ARRIVALS,)),
             pltpu.SemaphoreType.DMA((9,)),
         ],
         compiler_params=pltpu.CompilerParams(
@@ -559,8 +603,9 @@
         ),
         name="window",
     )(*args)
-    mean = 1.0 / (SLOTS * TOK)
-    return act.astype(BF16), grad.astype(BF16), *[total * mean for total in sums]
+    return pl.pallas_call(
+        hand_out, out_shape=out_shape, in_specs=[vmem], out_specs=(vmem,) * 6, name="hand_out"
+    )(packed)
 
 
 def solution(mesh):

time: 63 us -> 56.8 us (0.902)
  other arithmetic: 5.66 us -> 0 us
    convert_element_type x2 -> x0, other arithmetic: 3.04 us -> none  [the longest x1 1.52 us: local(): act.astype(BF16)]
    mul x2 -> x0, other arithmetic: 2.62 us -> none  [local(): total * mean]
    pallas_call x1 -> x2, Pallas kernels: 56.4 us -> 56 us  [the longest x1 54.4 us: local(): pl.pallas_call(kernel, out_shape=jax.ShapeDtypeStruct((168, COLS), F32),...]
where the time goes in v3:
time: 56.8 us; the launch traced here: 56.7 us
  Pallas kernels  56 us (99%)
  between operations  0.64 us (1%)
    pallas_call x1, Pallas kernels, local(): pl.pallas_call(kernel, out_shape=jax.ShapeDtypeStruct((168, COLS), F32),...  54.4 us
    pallas_call x1, Pallas kernels, local(): pl.pallas_call(hand_out, out_shape=out_shape, in_specs=[vmem], out_specs=...  1.61 us

profile of v3, /device:TPU:198, one launch (start us, length us, event | category | flops | bytes accessed | tf_op | source)
XLA Modules:
  0.0 56.7 jit_solution(15208642683974269558)
XLA Ops:
  0.6 54.4 %window.1.packed = f32[168,384]{1,0:T(8,128)} custom-call(bf16[1,64,384]{2,1,0:T(8,128)(2,1)} %act_hbm.1, bf16[1,64,384]{2,1,0:T(8,128)(2,1)} %ent_hbm.1, bf16[1,2,64,384]{3,2,1,0:T(8,128)(2,1)} %sta_hbm.1, bf16[1,64,384]{2,1,0:T(8,128)(2,1)} %tg_hbm.1, bf16[1,64,384]{2,1,0:T(8,128)(2,1)} %ret_hbm.1, bf16[1,6144,384]{2,1,0:T(8,128)(2,1)} %frozen_hbm.1, ...), custom_call_target="tpu_custom_call" | custom-call | tf_op jit(solution)/shard_map/window/pallas_call | solution.py:569
  55.1 1.6 %hand_out.1 = (bf16[1,64,384]{2,1,0:T(8,128)(2,1)}, bf16[1,64,384]{2,1,0:T(8,128)(2,1)}, f32[1,384]{1,0:T(1,128)}, f32[1,16,384]{2,1,0:T(8,128)}, f32[1,16,384]{2,1,0:T(8,128)}, /*index=5*/f32[1,384]{1,0:T(1,128)}) custom-call(f32[168,384]{1,0:T(8,128)} %window.1.packed), custom_call_target="tpu_custom_call" | custom-call | tf_op jit(solution)/shard_map/hand_out/pallas_call | solution.py:606

commit v4 on v3

--- a/solution.py
+++ b/solution.py
@@ -18,7 +18,7 @@
 FEATURES = CHIPS * PAIR
 SLOTS = 2
 ORDER = (3, 5, 4, 1, 7, 2, 6, 0)
-ARRIVALS = 90
+ARRIVALS = 94
 DEPARTURES = 30
 
 
@@ -148,8 +148,8 @@
     class Gather:
         groups = {0: (0,), 6: (6, 2), 2: (6, 2), 7: (7, 1), 1: (7, 1), 5: (5, 3, 4), 3: (5, 3, 4), 4: (5, 3, 4)}
 
-        def __init__(self, ref, rows, split, lead=None):
-            self.ref, self.rows, self.split, self.lead = ref, slice(0, rows), split, lead
+        def __init__(self, ref, rows, split, lead=None, deep=False):
+            self.ref, self.rows, self.split, self.lead, self.deep = ref, slice(0, rows), split, lead, deep
             self.near, self.far, self.lead_in = {}, {}, {}
             self.far4 = Arrival(ref.at[4, self.rows, mine])
             self.shared, self.lead_shared = {}, {}
@@ -164,8 +164,8 @@
         def lead_row(self, slot):
             return self.lead.at[slot, 0:1, mine]
 
-        def begin(self):
-            for offset in (2, -2, 1, -1):
+        def begin(self, offsets=(2, -2, 1, -1)):
+            for offset in offsets:
                 slot = (-offset) % CHIPS
                 if self.lead is not None:
                     self.lead_in[slot] = send(self.lead_row(0), self.lead_row(slot), chip(offset), kind=None)
@@ -174,7 +174,7 @@
                     self.share(0)
 
         def begin_next(self, src, first):
-            for offset in (2, -2, 0, 1, -1):
+            for offset in (0, 1, -1) if self.deep else (2, -2, 0, 1, -1):
                 slot = (-offset) % CHIPS
                 arrival = send(src, self.block(slot), following(offset), kind=2)
                 if offset == 0:
@@ -200,6 +200,23 @@
             send(self.block(slot), self.block(slot), sibling, self.shared[slot])
 
         def pass_on(self):
+            if self.deep:
+                for held, step in ((7, 1), (1, -1)):
+                    slot = (held - step) % CHIPS
+                    if self.lead is not None:
+                        self.lead_in[held].wait()
+                        self.lead_in[slot] = send(self.lead_row(held), self.lead_row(slot), chip(step), kind=None)
+                    self.near[held].wait()
+                    self.near[slot] = send(self.block(held), self.block(slot), chip(step))
+                    self.share(held)
+            else:
+                self.pass_far()
+
+        def pass_two(self):
+            if self.deep:
+                self.pass_far()
+
+        def pass_far(self):
             for held, step in ((6, 1), (2, -1)):
                 slot = (held - step) % CHIPS
                 if self.lead is not None:
@@ -214,7 +231,7 @@
                 self.share(held)
 
         def share_near(self):
-            for slot in (7, 1):
+            for slot in () if self.deep else (7, 1):
                 self.near[slot].wait()
                 if self.lead is not None:
                     self.lead_in[slot].wait()
@@ -289,11 +306,21 @@
                 self.pb[n] = result.astype(BF16)
             return send(self.pb.at[start:stop, :, other], self.sb.at[start:stop], sibling)
 
+        def part(self, start, stop):
+            arrival = self.compute(start, stop)
+            for n in range(start, stop):
+                self.halves[n] = arrival
+
         def compute_first(self):
-            self.first = self.compute(0, 3)
+            self.halves = {}
+            for n in (2, 0, 1):
+                self.part(n, n + 1)
+            self.part(3, 5)
+            self.stage_one()
 
         def compute_second(self):
-            self.second = self.compute(3, 8)
+            self.part(5, 8)
+            self.stage_one_direct()
 
         def pair_sum(self, n):
             return self.pb[n, :, mine].astype(F32) + self.sb[n].astype(F32)
@@ -307,28 +334,31 @@
 
         def stage_one(self):
             rv, sv = self.rv, self.sv
-            self.first.wait()
+            self.halves[2].wait()
             sv[2] = self.pair_sum(2).astype(BF16)
             low, high = slice(0, self.split), slice(self.split, self.rows)
             self.r4a = send(sv.at[2, low], rv.at[2, low], chip(-2))
             self.r4b = send(sv.at[2, high], rv.at[2, high], chip(2))
+            self.halves[0].wait()
             sv[0] = self.pair_sum(0).astype(BF16)
             self.r1 = send(sv.at[0], rv.at[0], chip(1))
+            self.halves[1].wait()
             sv[1] = self.pair_sum(1).astype(BF16)
             self.r2 = send(sv.at[1], rv.at[1], chip(-1))
 
         def stage_one_direct(self):
-            self.second.wait()
+            self.halves[3].wait()
             self.last = Arrival(self.rv.at[3:8] if self.back else self.rv.at[3:7])
             for n, offset in ((3, 1), (4, -1)):
                 self.sv[n] = self.pair_sum(n).astype(BF16)
                 self.deliver(n, offset)
+
+        def stage_two(self):
+            rv, split = self.rv, self.split
+            self.halves[5].wait()
             if self.back:
                 self.sv[7] = self.pair_sum(7).astype(BF16)
                 self.deliver(7, 0)
-
-        def stage_two(self):
-            rv, split = self.rv, self.split
             self.r1.wait()
             self.r4b.wait()
             total = self.pair_sum(5) + rv[0].astype(F32)
@@ -399,6 +429,7 @@
     norms = build(0, norms)
     squares, total = chunk(g0, 0, squares, total, True)
     ga_s0.pass_on()
+    ga_s0.pass_two()
     l_t0.wait()
     ga_t0.begin()
     ga_s0.share_near()
@@ -408,6 +439,7 @@
         squares, total = chunk(g0, slot, squares, total, True)
     ga_s0.share_far()
     ga_t0.pass_on()
+    ga_t0.pass_two()
     l_s1.wait()
     ga_s1.begin()
     for slot in (5, 3, 4):
@@ -429,13 +461,13 @@
     rs0.compute_second()
     ga_t0.share_near()
     ga_s1.pass_on()
-    rs0.stage_one()
+    ga_s1.pass_two()
     ga_t0.share_far()
     squares, total = fresh()
-    for slot in (0, 6, 2, 7, 1):
+    for slot in (0, 7, 1, 6, 2):
         ga_t0.ready(slot)
         squares, total = chunk(g1, slot, squares, total)
-    rs0.stage_one_direct()
+    rs0.stage_two()
     for slot in (5, 3, 4):
         ga_t0.ready(slot)
         squares, total = chunk(g1, slot, squares, total)
@@ -444,13 +476,12 @@
     l_ent.wait()
     ga_t1.begin_next(em, ent)
     ga_s1.share_near()
-    rs0.stage_two()
     normalise(g0, zn0, r0)
     factor = aout[...]
     weights0 = dot_nt(factor, pgs0)
     ga_s1.share_far()
     squares1, total1 = fresh()
-    for slot in (0, 6, 2, 7, 1):
+    for slot in (0, 7, 1, 6, 2):
         ga_s1.ready(slot)
         squares1, total1 = chunk(g2, slot, squares1, total1)
     for slot in (5, 3, 4):
@@ -463,6 +494,7 @@
     normalise(g2, zn1, r1)
     ga_t1.share_own(ent)
     ga_t1.pass_on()
+    ga_t1.pass_two()
     l_ret.wait()
 
     @pl.when(has_following)
@@ -491,9 +523,6 @@
     rs1.compute_first()
     rs1.compute_second()
     rows.compute()
-    rs1.stage_one()
-    rs1.stage_one_direct()
-    rows.stage_one()
     ga_t1.share_near()
     packed[160:168] = jnp.zeros((8, COLS), F32)
     packed[160:161] = inner / colnorm
@@ -506,13 +535,14 @@
     lower = (product - upper.astype(F32)).astype(BF16)
     both = dot(jnp.concatenate([upper, lower], axis=0), jnp.concatenate([pgs0, pgs1], axis=0))
     packed[144:160] = both[0:RANK] + both[RANK:] - adapter_direction * scaled_ratio
+    rows.stage_one()
+    rs1.stage_two()
+    rows.stage_two()
     squares, total = fresh()
-    for slot in (0, 6, 2, 7, 1):
+    for slot in (0, 7, 1, 6, 2):
         ga_t1.ready(slot)
         squares, total = chunk(g3, slot, squares, total)
     ga_t1.share_far()
-    rs1.stage_two()
-    rows.stage_two()
     for slot in (5, 3, 4):
         ga_t1.ready(slot)
         squares, total = chunk(g3, slot, squares, total)

time: 56.8 us -> 56.2 us (0.989)
  the two profiles are of different devices: /device:TPU:198 before, /device:TPU:256 now
where the time goes in v4:
time: 56.2 us; the launch traced here: 56 us
  Pallas kernels  55.4 us (99%)
  between operations  0.64 us (1%)
    pallas_call x1, Pallas kernels, local(): pl.pallas_call(kernel, out_shape=jax.ShapeDtypeStruct((168, COLS), F32),...  53.7 us
    pallas_call x1, Pallas kernels, local(): pl.pallas_call(hand_out, out_shape=out_shape, in_specs=[vmem], out_specs=...  1.61 us

profile of v4, /device:TPU:256, one launch (start us, length us, event | category | flops | bytes accessed | tf_op | source)
XLA Modules:
  0.0 56.0 jit_solution(13027965508741380059)
XLA Ops:
  0.6 53.7 %window.1.packed = f32[168,384]{1,0:T(8,128)} custom-call(bf16[1,64,384]{2,1,0:T(8,128)(2,1)} %act_hbm.1, bf16[1,64,384]{2,1,0:T(8,128)(2,1)} %ent_hbm.1, bf16[1,2,64,384]{3,2,1,0:T(8,128)(2,1)} %sta_hbm.1, bf16[1,64,384]{2,1,0:T(8,128)(2,1)} %tg_hbm.1, bf16[1,64,384]{2,1,0:T(8,128)(2,1)} %ret_hbm.1, bf16[1,6144,384]{2,1,0:T(8,128)(2,1)} %frozen_hbm.1, ...), custom_call_target="tpu_custom_call" | custom-call | tf_op jit(solution)/shard_map/window/pallas_call | solution.py:599
  54.4 1.6 %hand_out.1 = (bf16[1,64,384]{2,1,0:T(8,128)(2,1)}, bf16[1,64,384]{2,1,0:T(8,128)(2,1)}, f32[1,384]{1,0:T(1,128)}, f32[1,16,384]{2,1,0:T(8,128)}, f32[1,16,384]{2,1,0:T(8,128)}, /*index=5*/f32[1,384]{1,0:T(1,128)}) custom-call(f32[168,384]{1,0:T(8,128)} %window.1.packed), custom_call_target="tpu_custom_call" | custom-call | tf_op jit(solution)/shard_map/hand_out/pallas_call | solution.py:636

commit v5 on v4

--- a/solution.py
+++ b/solution.py
@@ -18,8 +18,8 @@
 FEATURES = CHIPS * PAIR
 SLOTS = 2
 ORDER = (3, 5, 4, 1, 7, 2, 6, 0)
-ARRIVALS = 94
-DEPARTURES = 30
+ARRIVALS = 89
+DEPARTURES = 27
 
 
 def dot(a, b):
@@ -42,9 +42,9 @@
 
 
 def kernel(
-    act_hbm, ent_hbm, sta_hbm, tg_hbm, ret_hbm, frozen_hbm, ain_hbm, aout_hbm, mag_ref, gain_ref,
+    act_hbm, ent_hbm, sta_hbm, tg_hbm, ret_hbm, frozen_hbm, ain_hbm, aout_hbm, mag_hbm, gain_hbm,
     packed,
-    fz, w, g0, g1, g2, g3, gn, zn0, zn1, tg, tgx, ent, ret, aout, em, gx,
+    mag, gain_row, fz, w, g0, g1, g2, g3, gn, zn0, zn1, tg, tgx, ent, ret, aout, em, gx,
     pb0, sb0, sv0, rv0, pb1, sb1, sv1, rv1, gt, gts, gtv, gtr, ssem, rsem, lsem,
 ):
     me = lax.axis_index("tensor")
@@ -113,6 +113,8 @@
         locals_.append(copy)
         return copy
 
+    l_gain = load(gain_hbm, gain_row)
+    l_mag = load(mag_hbm, mag)
     l_s0 = load(sta_hbm.at[0, 0], g0.at[0, 0:TOK, mine])
     l_a = load(ain_hbm.at[0], g0.at[0, TOK : TOK + RANK, mine])
     l_fz = load(frozen_hbm.at[0], fz)
@@ -134,15 +136,16 @@
 
     @pl.when(has_previous)
     def _():
-        greet([previous(offset) for offset in near])
+        greet([previous(0)])
 
     @pl.when(has_following)
     def _():
-        greet([following(offset) for offset in near])
-
-    gain = gain_ref[...].astype(F32)
+        greet([following(0)])
+
+    l_gain.wait()
+    gain = gain_row[...].astype(F32)
     gn[0, 0:1, mine] = gain
-    expected = len(near) * (1 + jnp.where(has_following, 1, 0) + jnp.where(has_previous, 1, 0))
+    expected = len(near) + jnp.where(has_following, 1, 0) + jnp.where(has_previous, 1, 0)
     pl.semaphore_wait(barrier, expected)
 
     class Gather:
@@ -448,7 +451,8 @@
         squares, total = chunk(g0, slot, squares, total, True)
     norm_squares = jnp.sum(norms, axis=0, keepdims=True) + 1e-06
     colnorm = jnp.sqrt(norm_squares)
-    col_scale = mag_ref[...] / colnorm
+    l_mag.wait()
+    col_scale = mag[...] / colnorm
     r0 = rscale_of(squares)
     raw0 = total[0:TOK] * r0
     adapter_direction = total[TOK:]
@@ -599,9 +603,11 @@
     packed = pl.pallas_call(
         kernel,
         out_shape=jax.ShapeDtypeStruct((168, COLS), F32),
-        in_specs=[hbm] * 8 + [vmem] * 2,
+        in_specs=[hbm] * 10,
         out_specs=vmem,
         scratch_shapes=[
+            pltpu.VMEM((1, COLS), F32),
+            pltpu.VMEM((1, COLS), BF16),
             pltpu.VMEM((FEATURES, COLS), BF16),
             pltpu.VMEM((FEATURES, COLS), BF16),
             pltpu.VMEM((CHIPS, rows1, PAIR), BF16),
@@ -626,7 +632,7 @@
             pltpu.VMEM((8, COLS), F32),
             pltpu.SemaphoreType.DMA((DEPARTURES,)),
             pltpu.SemaphoreType.DMA((ARRIVALS,)),
-            pltpu.SemaphoreType.DMA((9,)),
+            pltpu.SemaphoreType.DMA((11,)),
         ],
         compiler_params=pltpu.CompilerParams(
             collective_id=0, has_side_effects=True, vmem_limit_bytes=56 * 2**20

time: 56.2 us -> 54.7 us (0.973)
  Pallas kernels: 55.4 us -> 53.9 us
    pallas_call x1, Pallas kernels: 53.7 us -> 52.3 us  [local(): pl.pallas_call(kernel, out_shape=jax.ShapeDtypeStruct((168, COLS), F32),...]
where the time goes in v5:
time: 54.7 us; the launch traced here: 54.6 us
  Pallas kernels  53.9 us (99%)
  between operations  0.64 us (1%)
    pallas_call x1, Pallas kernels, local(): pl.pallas_call(kernel, out_shape=jax.ShapeDtypeStruct((168, COLS), F32),...  52.3 us
    pallas_call x1, Pallas kernels, local(): pl.pallas_call(hand_out, out_shape=out_shape, in_specs=[vmem], out_specs=...  1.61 us

profile of v5, /device:TPU:256, one launch (start us, length us, event | category | flops | bytes accessed | tf_op | source)
XLA Modules:
  0.0 54.6 jit_solution(10240547529772242896)
XLA Ops:
  0.6 52.3 %window.1.packed = f32[168,384]{1,0:T(8,128)} custom-call(bf16[1,64,384]{2,1,0:T(8,128)(2,1)} %act_hbm.1, bf16[1,64,384]{2,1,0:T(8,128)(2,1)} %ent_hbm.1, bf16[1,2,64,384]{3,2,1,0:T(8,128)(2,1)} %sta_hbm.1, bf16[1,64,384]{2,1,0:T(8,128)(2,1)} %tg_hbm.1, bf16[1,64,384]{2,1,0:T(8,128)(2,1)} %ret_hbm.1, bf16[1,6144,384]{2,1,0:T(8,128)(2,1)} %frozen_hbm.1, ...), custom_call_target="tpu_custom_call" | custom-call | tf_op jit(solution)/shard_map/window/pallas_call | solution.py:603
  53.0 1.6 %hand_out.1 = (bf16[1,64,384]{2,1,0:T(8,128)(2,1)}, bf16[1,64,384]{2,1,0:T(8,128)(2,1)}, f32[1,384]{1,0:T(1,128)}, f32[1,16,384]{2,1,0:T(8,128)}, f32[1,16,384]{2,1,0:T(8,128)}, /*index=5*/f32[1,384]{1,0:T(1,128)}) custom-call(f32[168,384]{1,0:T(8,128)} %window.1.packed), custom_call_target="tpu_custom_call" | custom-call | tf_op jit(solution)/shard_map/hand_out/pallas_call | solution.py:642
